TPU v7x, 128 devices: a whole 4x4x4 slice. The times are simulated.
128 devices in a mesh: leaf: 16 (over z, x), sub: 8 (over y, core).
Axes of the slice: x: 4, y: 4, z: 4, core: 2. Of those that a mesh axis runs over, the one named last changes fastest.
Arguments:
- points: float32 [131072, 64], P(('leaf', 'sub')), may hold values from -6 to 6
- leaf_maps: float32 [256, 128, 512], P(('leaf', 'sub')), may hold values from -0.25 to 0.25
- root_maps: float32 [256, 128, 512], P(('leaf', 'sub')), may hold values from -0.25 to 0.25
- current: float32 [131072], P(('leaf', 'sub')), may hold values from -6 to 6
- krylov_basis: float32 [8, 131072], P(None, ('leaf', 'sub')), may hold values from -0.015625 to 0.015625
- ritz_roots: float32 [2], replicated, may hold values from 40 to 400
- point_order: int32 [131072], P(('leaf', 'sub')), may hold values from 0 to 8191, as said below
- skeleton: int32 [256, 128], P(('leaf', 'sub')), may hold values from 0 to 511, as said below
- root_skeleton: int32 [16, 128], P('leaf'), may hold values from 0 to 8191, as said below
- near_list: int32 [256, 32], P(('leaf', 'sub')), may hold values from 0 to 47, as said below
- far_list: int32 [256, 4], P(('leaf', 'sub')), may hold values from 0 to 47, as said below
Outputs:
- orthogonal: float32 [131072], P(('leaf', 'sub'))
- hessenberg: float32 [9], replicated
Inputs may be any that keep to these rules, and one draw needn't show every extreme that they name: Within each subtree (block of 8192 tree positions) point_order is a permutation of 0 to 8191. `skeleton`: each row holds 128 different point numbers of the leaf. `root_skeleton`: each row holds 128 different point numbers of the subtree. `near_list`: slots count 16 leaves of the previous subtree, then the own subtree, then the next one (circularly). The first slot of leaf a is its own, 16 + (a mod 16); the slots of a row are different, and no slot of a row is in the leaf's far_list. `far_list`: slots as in near_list; different within a row, never the leaf's own.
All inputs are finite; a program needn't handle non-finite values.
Results may differ from a plain program's by a relative error of at most 0.000096.
Values sent between devices are 32-bit elements; how exact they have to be, the bound alone decides.
No kernel may reach another device: no remote copies, remote signals or barrier semaphores. Data moves between devices by JAX's collectives and lax.ppermute only.
A program may use at most 64 MiB of HBM per device.

v0:
```python
import jax
import jax.numpy as jnp
from jax import lax
from jax.sharding import PartitionSpec as P

HIGHEST_PREC = lax.Precision.HIGHEST
RIDGE_SHIFT = 1.0
EPSILON = 1e-06


def with_halo(block, sides, width):
    for axis, dim in sides:
        count = lax.axis_size(axis)
        forward = [(i, i + 1) for i in range(count - 1)]
        forward.append((count - 1, 0))
        backward = [(target, source) for source, target in forward]
        low = lax.ppermute(
            lax.slice_in_dim(block, block.shape[dim] - width, None, axis=dim), axis, forward
        )
        high = lax.ppermute(lax.slice_in_dim(block, 0, width, axis=dim), axis, backward)
        block = jnp.concatenate([low, block, high], axis=dim)
    return block


def gaussian(inner_prod, target_sq, source_sq, feat_count):
    return jnp.exp(-(target_sq + source_sq - 2.0 * inner_prod) / feat_count)


def shards(
    points,
    leaf_maps,
    root_maps,
    current,
    krylov_basis,
    ritz_roots,
    point_order,
    skeleton,
    root_skeleton,
    near_list,
    far_list,
):
    per_device, skel_count, leaf_size = leaf_maps.shape
    feat_count = points.shape[1]
    sub_count = lax.axis_size("sub")
    sub_leaves = per_device * sub_count
    leaf_count = lax.axis_size("leaf")
    leaf_index = lax.axis_index("leaf")
    own_points = points.reshape(per_device, leaf_size, feat_count)
    own_sq = jnp.sum(own_points * own_points, axis=-1)
    skel_points = jnp.take_along_axis(own_points, skeleton[:, :, None], axis=1)
    skel_sq = jnp.sum(skel_points * skel_points, axis=-1)
    leaf_data = jnp.concatenate([own_points, skel_points], axis=1)
    subtree_data = lax.all_gather(leaf_data, "sub", axis=0, tiled=True)
    window_data = with_halo(subtree_data, (("leaf", 0),), sub_leaves)
    window_points = window_data[:, :leaf_size]
    window_sq = jnp.sum(window_points * window_points, axis=-1)
    far_points = window_data[far_list][:, :, leaf_size:]
    far_inner = jnp.einsum("bmf,bjnf->bjmn", skel_points, far_points, precision=HIGHEST_PREC)
    far_kernel = gaussian(
        far_inner,
        skel_sq[:, None, :, None],
        jnp.sum(far_points * far_points, axis=-1)[:, :, None, :],
        feat_count,
    )
    subtree_points = window_points[sub_leaves : 2 * sub_leaves].reshape(
        sub_leaves * leaf_size, feat_count
    )
    own_root = jnp.take(subtree_points, root_skeleton[0], axis=0)
    all_roots = lax.all_gather(own_root[None], "leaf", axis=0, tiled=True).reshape(
        leaf_count * skel_count, feat_count
    )
    own_root_sq = jnp.sum(own_root * own_root, axis=-1)
    all_root_sq = jnp.sum(all_roots * all_roots, axis=-1)
    top_inner = jnp.dot(own_root, all_roots.T, precision=HIGHEST_PREC)
    top_kernel = gaussian(top_inner, own_root_sq[:, None], all_root_sq[None, :], feat_count)
    distance = (jnp.arange(leaf_count, dtype=jnp.int32) - leaf_index) % leaf_count
    far_mask = (distance >= 1).astype(jnp.float32)
    top_kernel = top_kernel * jnp.repeat(far_mask, skel_count)[None, :]
    near_count = near_list.shape[1]
    neighbour_pairs = near_list.reshape(per_device, near_count // 2, 2).transpose(1, 0, 2)

    def operator(vector):
        values = vector.reshape(per_device, leaf_size)
        skel_weights = jnp.einsum("bkn,bn->bk", leaf_maps, values, precision=HIGHEST_PREC)
        root_part = jnp.einsum("bkn,bn->k", root_maps, values, precision=HIGHEST_PREC)
        packed = jnp.concatenate([values, skel_weights], axis=1)
        subtree_values = lax.all_gather(packed, "sub", axis=0, tiled=True)
        window_values = with_halo(subtree_values, (("leaf", 0),), sub_leaves)
        root_total = lax.psum(root_part, "sub")
        root_weights = lax.all_gather(root_total[None], "leaf", axis=0, tiled=True)
        window_entries = window_values[:, :leaf_size]

        def near_step(running, indices):
            sources = window_points[indices]
            inner_prod = jnp.einsum("bmf,bjnf->bjmn", own_points, sources, precision=HIGHEST_PREC)
            kernel = gaussian(
                inner_prod, own_sq[:, None, :, None], window_sq[indices][:, :, None, :], feat_count
            )
            return (
                running
                + jnp.einsum(
                    "bjmn,bjn->bm", kernel, window_entries[indices], precision=HIGHEST_PREC
                ),
                None,
            )

        start_sum = jnp.zeros((per_device, leaf_size), jnp.float32)
        result, leftover = lax.scan(near_step, start_sum, neighbour_pairs)
        skel_out = jnp.einsum(
            "bjmn,bjn->bm",
            far_kernel,
            window_values[far_list][:, :, leaf_size:],
            precision=HIGHEST_PREC,
        )
        result = result + jnp.einsum("bkn,bk->bn", leaf_maps, skel_out, precision=HIGHEST_PREC)
        root_out = jnp.dot(top_kernel, root_weights.reshape(-1), precision=HIGHEST_PREC)
        result = result + jnp.einsum("bkn,k->bn", root_maps, root_out, precision=HIGHEST_PREC)
        return result.reshape(-1) + RIDGE_SHIFT * vector

    user_subtree = lax.all_gather(current, "sub", axis=0, tiled=True)
    tree_vector = jnp.take(user_subtree, point_order, axis=0)
    first_section = tree_vector - operator(tree_vector) / ritz_roots[0]
    second = first_section - operator(first_section) / ritz_roots[1]
    preconditioned = tree_vector - second
    placed = jnp.zeros((sub_leaves * leaf_size,), jnp.float32).at[point_order].set(preconditioned)
    user_grown = lax.psum_scatter(placed, "sub", scatter_dimension=0, tiled=True)
    local_proj = jnp.dot(krylov_basis, user_grown, precision=HIGHEST_PREC)
    projections = lax.psum(local_proj, ("leaf", "sub"))
    orthogonal = user_grown - jnp.dot(projections, krylov_basis, precision=HIGHEST_PREC)
    length_sq = lax.psum(jnp.sum(orthogonal * orthogonal), ("leaf", "sub"))
    length_norm = jnp.sqrt(length_sq + EPSILON)
    return (orthogonal, jnp.concatenate([projections, length_norm[None]]))


def solution(mesh):
    return jax.shard_map(
        shards,
        mesh=mesh,
        in_specs=(
            P(("leaf", "sub"), None),
            P(("leaf", "sub"), None, None),
            P(("leaf", "sub"), None, None),
            P(("leaf", "sub")),
            P(None, ("leaf", "sub")),
            P(),
            P(("leaf", "sub")),
            P(("leaf", "sub"), None),
            P("leaf", None),
            P(("leaf", "sub"), None),
            P(("leaf", "sub"), None),
        ),
        out_specs=(P(("leaf", "sub")), P()),
        check_vma=False,
    )
```

profile of v0, /device:TPU:1, one launch (start us, length us, event | category | flops | bytes accessed | tf_op | source)
XLA Modules:
  0.0 843.7 jit_solution(11445859669285656474)
XLA Ops:
  13.6 14.6 %all_gather.21 = f32[8192]{0:T(1024)S(1)} all-gather(f32[1024]{0:T(1024)S(1)} %copy-done.9), channel_id=1, replica_groups=mesh['leaf'=16,'sub'=8] {'sub'}, dimensions={0}, use_global_device_ids=true | all-gather | bytes 36864 | tf_op jit(solution)/shard_map/all_gather | solution.py:120
  28.8 6.1 gather_fusion.6
  35.5 12.8 %all-gather = f32[8,2,640]{2,1,0:T(2,128)S(1)} all-gather(f32[1,2,640]{2,1,0:T(2,128)S(1)} %maximum_bitcast_fusion), channel_id=1, replica_groups=mesh['leaf'=16,'sub'=8] {'sub'}, dimensions={0}, use_global_device_ids=true | all-gather | bytes 46080 | tf_op jit(solution)/shard_map/all_gather | solution.py:87
  48.4 6.0 collective-permute-start.3
  64.5 13.2 %psum.28 = f32[1,128]{1,0:T(1,128)S(1)} all-reduce(f32[1,128]{1,0:T(1,128)S(1)} %convolution_bitcast_fusion.6), channel_id=1, replica_groups=mesh['leaf'=16,'sub'=8] {'sub'}, use_global_device_ids=true, to_apply=%region_8.9 | all-reduce | flops 128 | bytes 1024 | tf_op jit(solution)/shard_map/psum | solution.py:89
  77.7 50.0 %all-gather.1 = f32[16,1,128]{2,1,0:T(1,128)S(1)} all-gather(f32[1,1,128]{2,1,0:T(1,128)S(1)} %bitcast.264), channel_id=1, replica_groups=mesh['leaf'=16,'sub'=8] {'leaf'}, dimensions={0}, use_global_device_ids=true | all-gather | bytes 8704 | tf_op jit(solution)/shard_map/all_gather | solution.py:90
  137.6 16.9 %all_gather.24 = f32[16,128,64]{1,2,0:T(8,128)S(1)} all-gather(f32[1,128,64]{1,2,0:T(8,128)S(1)} %copy.45), channel_id=1, replica_groups=mesh['leaf'=16,'sub'=8] {'leaf'}, dimensions={0}, use_global_device_ids=true | all-gather | bytes 557056 | tf_op jit(solution)/shard_map/all_gather | solution.py:69
  171.5 7.0 fusion.62
  180.4 9.7 %copy.41 = f32[48,512,64]{2,1,0:T(8,128)} copy(f32[48,512,64]{1,2,0:T(8,128)} %get-tuple-element.242) | data formatting | bytes 12582912
  190.2 211.7 %while.22 = (s32[]{:T(128)}, f32[2,512]{1,0:T(2,128)S(1)}, f32[2,512]{1,0:T(2,128)S(1)}, s32[16,2,2]{2,1,0:T(2,128)S(1)}, f32[48,512]{1,0:T(8,128)S(1)}, /*index...) while((s32[]{:T(128)}, f32[2,512]{1,0:T(2,128)S(1)}, ...), condition=%wide.region_3.4_spmd.clone, body=%wide.region_2.3_spmd.clone.sunk | while | flops 823135232 | bytes 10330363 | solution.py:108
  204.7 5.2 gather_fusion.1
  217.9 5.2 gather_fusion.1
  231.1 5.2 gather_fusion.1
  257.6 5.2 gather_fusion.1
  284.1 5.2 gather_fusion.1
  297.3 5.2 gather_fusion.1
  310.5 5.2 gather_fusion.1
  323.8 5.2 gather_fusion.1
  337.0 5.2 gather_fusion.1
  350.2 5.2 gather_fusion.1
  363.5 5.2 gather_fusion.1
  376.7 5.2 gather_fusion.1
  403.6 22.1 %all-gather.2 = f32[8,2,640]{2,1,0:T(2,128)S(1)} all-gather(f32[1,2,640]{2,1,0:T(2,128)S(1)} %maximum_bitcast_fusion.1), channel_id=1, replica_groups=mesh['leaf'=16,'sub'=8] {'sub'}, dimensions={0}, use_global_device_ids=true | all-gather | bytes 46080 | tf_op jit(solution)/shard_map/all_gather | solution.py:87
  428.2 12.2 %psum.29 = f32[1,128]{1,0:T(1,128)S(1)} all-reduce(f32[1,128]{1,0:T(1,128)S(1)} %convolution_bitcast_fusion.5), channel_id=1, replica_groups=mesh['leaf'=16,'sub'=8] {'sub'}, use_global_device_ids=true, to_apply=%region_11.12 | all-reduce | flops 128 | bytes 1024 | tf_op jit(solution)/shard_map/psum | solution.py:89
  440.4 17.4 %all-gather.3 = f32[16,1,128]{2,1,0:T(1,128)S(1)} all-gather(f32[1,1,128]{2,1,0:T(1,128)S(1)} %bitcast.265), channel_id=1, replica_groups=mesh['leaf'=16,'sub'=8] {'leaf'}, dimensions={0}, use_global_device_ids=true | all-gather | bytes 8704 | tf_op jit(solution)/shard_map/all_gather | solution.py:90
  461.4 212.0 %while.23 = (s32[]{:T(128)}, f32[2,512]{1,0:T(2,128)S(1)}, f32[2,512]{1,0:T(2,128)S(1)}, s32[16,2,2]{2,1,0:T(2,128)S(1)}, f32[48,512]{1,0:T(8,128)S(1)}, /*index...) while((s32[]{:T(128)}, f32[2,512]{1,0:T(2,128)S(1)}, ...), condition=%wide.region_10.11_spmd.clone, body=%wide.region_9.10_spmd.clone.sunk | while | flops 823135232 | bytes 10330363 | solution.py:108
  463.0 5.2 gather_fusion.4
  476.2 5.2 gather_fusion.4
  502.7 5.2 gather_fusion.4
  679.5 26.8 %all-reduce = f32[8192]{0:T(1024)S(1)} all-reduce(f32[8192]{0:T(1024)S(1)} %scatter_custom_fusion), channel_id=2, replica_groups=mesh['leaf'=16,'sub'=8] {'sub'}, use_global_device_ids=true, to_apply=%region_13.14.clone | all-reduce | flops 8192 | bytes 65536
  706.4 65.3 %psum.30 = f32[8]{0:T(128)S(1)} all-reduce(f32[8]{0:T(128)S(1)} %convolution_bitcast_fusion.4), channel_id=1, replica_groups=mesh['leaf'=16,'sub'=8] {'leaf','sub'}, use_global_device_ids=true, to_apply=%region_14.15 | all-reduce | flops 8 | bytes 64 | tf_op jit(solution)/shard_map/psum | solution.py:128
  773.0 62.5 %psum.31 = f32[]{:T(128)} all-reduce(f32[]{:T(128)} %get-tuple-element.238), channel_id=1, replica_groups=mesh['leaf'=16,'sub'=8] {'leaf','sub'}, use_global_device_ids=true, to_apply=%region_16.17 | all-reduce | flops 1 | bytes 8 | tf_op jit(solution)/shard_map/psum | solution.py:130
  (467 shorter events, 405.5 us)
Async XLA Ops:
  7.2 27.8 %copy-start = (f32[2,128,512]{2,1,0:T(8,128)S(1)}, f32[2,128,512]{2,1,0:T(8,128)}, u32[]{:S(2)}) copy-start(f32[2,128,512]{2,1,0:T(8,128)} %param.16) | copy-start | bytes 1572868
  7.2 6.4 copy-start.9
  7.2 21.0 %copy-start.8 = (s32[1024]{0:T(1024)S(1)}, s32[1024]{0:T(1024)}, u32[]{:S(2)}) copy-start(s32[1024]{0:T(1024)} %param.21) | copy-start | bytes 12292
  7.2 47.9 %all-gather.6.cloned.1.call-start = ((), (), s32[]{:S(2)}) async-start(), calls=%async_computation | async-start | bytes 2949120 | tf_op jit(solution)/shard_map/all_gather | solution.py:53
  11.7 42.7 %copy-start.14 = (s32[2,4]{1,0:T(2,128)S(1)}, s32[2,4]{1,0:T(2,128)}, u32[]{:S(2)}) copy-start(s32[2,4]{1,0:T(2,128)} %param.25) | copy-start | bytes 100
  11.7 42.8 %copy-start.12 = (f32[2]{0:T(128)S(1)}, f32[2]{0:T(128)}, u32[]{:S(2)}) copy-start(f32[2]{0:T(128)} %param.20) | copy-start | bytes 28
  11.7 43.3 %copy-start.6 = (f32[1024,64]{0,1:T(8,128)S(1)}, f32[1024,64]{0,1:T(8,128)}, u32[]{:S(2)}) copy-start(f32[1024,64]{0,1:T(8,128)} %param.15) | copy-start | bytes 786436
  11.8 43.5 %copy-start.2 = (f32[2,128,512]{2,1,0:T(8,128)S(1)}, f32[2,128,512]{2,1,0:T(8,128)}, u32[]{:S(2)}) copy-start(f32[2,128,512]{2,1,0:T(8,128)} %param.17) | copy-start | bytes 1572868
  12.5 1.0 copy-start.4
  12.5 43.2 %copy-start.15 = (s32[1,128]{1,0:T(1,128)S(1)}, s32[1,128]{1,0:T(1,128)}, u32[]{:S(2)}) copy-start(s32[1,128]{1,0:T(1,128)} %param.23) | copy-start | bytes 1540
  12.6 50.7 %copy-start.13 = (s32[2,32]{1,0:T(2,128)S(1)}, s32[2,32]{1,0:T(2,128)}, u32[]{:S(2)}) copy-start(s32[2,32]{1,0:T(2,128)} %param.24) | copy-start | bytes 772
  12.6 50.8 %copy-start.16 = (u32[128]{0:T(128)S(1)}, u32[128]{0:T(128)}, u32[]{:S(2)}) copy-start(u32[128]{0:T(128)} %constant.132) | copy-start | bytes 1540
  48.4 79.4 %collective-permute-start.3 = (f32[16,640]{1,0:T(8,128)S(1)}, f32[16,640]{1,0:T(8,128)S(1)}, u32[]{:S(2)}, u32[]{:S(2)}) collective-permute-start(f32[16,640]{1,0:T(8,128)S(1)} %reshape.306), channel_id=1, source_target_pairs={{8,0},{16,8},{24,16},{32,24},{40,32},{48,40},{56,48},{64,56},{72,6... | collective-permute-start | bytes 122888 | tf_op jit(solution)/shard_map/ppermute | solution.py:20
  54.4 73.3 %collective-permute-start.2 = (f32[16,640]{1,0:T(8,128)S(1)}, f32[16,640]{1,0:T(8,128)S(1)}, u32[]{:S(2)}, u32[]{:S(2)}) collective-permute-start(f32[16,640]{1,0:T(8,128)S(1)} %reshape.306), channel_id=1, source_target_pairs={{0,8},{8,16},{16,24},{24,32},{32,40},{40,48},{48,56},{56,64},{64,7... | collective-permute-start | bytes 122888 | tf_op jit(solution)/shard_map/ppermute | solution.py:17
  55.2 103.7 %collective-permute-start = (f32[16,640,64]{1,2,0:T(8,128)}, f32[16,640,64]{1,2,0:T(8,128)}, u32[]{:S(2)}, u32[]{:S(2)}) collective-permute-start(f32[16,640,64]{1,2,0:T(8,128)} %all-gather.6.cloned.1.call-done), channel_id=1, source_target_pairs={{0,8},{8,16},{16,24},{24,32},{32,40},{40,48},{48,56},{56,64},{64,7... | collective-permute-start | bytes 7864328 | tf_op jit(solution)/shard_map/ppermute | solution.py:17
  56.4 107.8 %collective-permute-start.1 = (f32[16,640,64]{1,2,0:T(8,128)}, f32[16,640,64]{1,2,0:T(8,128)}, u32[]{:S(2)}, u32[]{:S(2)}) collective-permute-start(f32[16,640,64]{1,2,0:T(8,128)} %all-gather.6.cloned.1.call-done), channel_id=1, source_target_pairs={{8,0},{16,8},{24,16},{32,24},{40,32},{48,40},{56,48},{64,56},{72,6... | collective-permute-start | bytes 7864328 | tf_op jit(solution)/shard_map/ppermute | solution.py:20
  154.5 7.9 copy-start.1
  156.6 1.0 copy-start.3
  171.5 7.1 copy-start.5
  171.5 7.1 copy-start.11
  180.4 9.7 %copy-start.10 = (f32[2,512]{1,0:T(2,128)S(1)}, f32[2,512]{1,0:T(2,128)}, u32[]{:S(2)}) copy-start(f32[2,512]{1,0:T(2,128)} %reduce_sum.66) | copy-start | bytes 12292
  425.7 34.7 %collective-permute-start.5 = (f32[16,640]{1,0:T(8,128)S(1)}, f32[16,640]{1,0:T(8,128)S(1)}, u32[]{:S(2)}, u32[]{:S(2)}) collective-permute-start(f32[16,640]{1,0:T(8,128)S(1)} %reshape.310), channel_id=1, source_target_pairs={{8,0},{16,8},{24,16},{32,24},{40,32},{48,40},{56,48},{64,56},{72,6... | collective-permute-start | bytes 122888 | tf_op jit(solution)/shard_map/ppermute | solution.py:20
  428.2 32.2 %collective-permute-start.4 = (f32[16,640]{1,0:T(8,128)S(1)}, f32[16,640]{1,0:T(8,128)S(1)}, u32[]{:S(2)}, u32[]{:S(2)}) collective-permute-start(f32[16,640]{1,0:T(8,128)S(1)} %reshape.310), channel_id=1, source_target_pairs={{0,8},{8,16},{16,24},{24,32},{32,40},{40,48},{48,56},{56,64},{64,7... | collective-permute-start | bytes 122888 | tf_op jit(solution)/shard_map/ppermute | solution.py:17
  461.4 244.8 %copy-start.7 = (f32[8,1024]{1,0:T(8,128)S(1)}, f32[8,1024]{1,0:T(8,128)}, u32[]{:S(2)}) copy-start(f32[8,1024]{1,0:T(8,128)} %param.19) | copy-start | bytes 98308
Sparse Core Ops, SparseCore 0:
  13.7 29.7 all-gather.5
where the time goes:
time: 846 us; the launch traced here: 844 us
  blocking collectives  314 us (37%)
  local copies, waits for them, and re-layouts  256 us (30%)
  matrix products  226 us (27%)
  other arithmetic  17.4 us (2%)
  between operations  15.8 us (2%)
  starting transfers between devices  13.4 us (2%)
    gather x32, local copies, waits for them, and re-layouts, near_step(): sources = window_points[indices]  166 us
    dot_general x32, matrix products, near_step(): jnp.einsum('bmf,bjnf->bjmn', own_points, sources, precision=HIGHEST_PREC)  115 us
    dot_general x32, matrix products, near_step(): jnp.einsum('bjmn,bjn->bm', kernel, window_entries[indices], precision=HIG...  100 us
    all_gather x2, blocking collectives, operator(): root_weights = lax.all_gather(root_total[None], 'leaf', axis=0, tiled=True)  67.4 us
    psum x1, blocking collectives, shards(): projections = lax.psum(local_proj, ('leaf', 'sub'))  65.3 us
    psum x1, blocking collectives, shards(): length_sq = lax.psum(jnp.sum(orthogonal * orthogonal), ('leaf', 'sub'))  62.5 us
    all_gather x2, blocking collectives, operator(): subtree_values = lax.all_gather(packed, 'sub', axis=0, tiled=True)  35 us
    unnamed x1, blocking collectives  26.8 us
  transfers between devices with their start and end apart: 7, of which 0 were waited for; matrix products, arithmetic and copies ran while one was open for 4% of the time, Pallas kernels for 0%

commit v1 on v0

v1 whole, which is shorter than its diff:
```python
import functools
import math

import jax
import jax.numpy as jnp
from jax import lax
from jax.experimental import pallas as pl
from jax.experimental.pallas import tpu as pltpu
from jax.sharding import PartitionSpec as P

F32 = jnp.float32
BF16 = jnp.bfloat16
HI = lax.Precision.HIGHEST
RIDGE = 1.0
EPSILON = 1e-06
LANES = 128
BOTH = ("leaf", "sub")
VMEM_LIMIT = 50 * 1024 * 1024
NT = (((1,), (1,)), ((), ()))
TN = (((0,), (0,)), ((), ()))


def dot(a, b, dims=(((1,), (0,)), ((), ())), precision=None):
    return lax.dot_general(a, b, dims, precision=precision, preferred_element_type=F32)


def halves(x):
    h = x.astype(BF16)
    return h, (x - h.astype(F32)).astype(BF16)


def thirds(x):
    a = x.astype(BF16)
    r = x - a.astype(F32)
    b = r.astype(BF16)
    return a, b, (r - b.astype(F32)).astype(BF16)


def row_sums(block):
    return dot(jnp.ones((8, LANES), F32), block, NT, HI)[:1]


def half_norm(h, l):
    x = h.astype(F32) + l.astype(F32)
    return jnp.exp2(-0.5 * jnp.sum(x * x, axis=0, keepdims=True))


def pick(index_row, count):
    shape = (count, index_row.shape[1])
    return lax.broadcasted_iota(jnp.int32, shape, 0) == jnp.broadcast_to(index_row, shape)


def split_order(order):
    row = (lax.shift_right_logical(order, 7) & 7) * 8 + lax.shift_right_logical(order, 10)
    return row, order & 127


def call(body, outs, *args, smem=(), scratch=(), cost=None, name=None):
    specs = [
        pl.BlockSpec(memory_space=pltpu.SMEM if i in smem else pltpu.VMEM) for i in range(len(args))
    ]
    return pl.pallas_call(
        body,
        out_shape=outs,
        in_specs=specs,
        out_specs=[pl.BlockSpec(memory_space=pltpu.VMEM)] * len(outs),
        scratch_shapes=list(scratch),
        compiler_params=pltpu.CompilerParams(vmem_limit_bytes=VMEM_LIMIT),
        cost_estimate=cost,
        name=name,
    )(*args)


def prepare_kernel(
    scale, leaf_size, pts, qt, skel, rskel, cur, basis, lhs, u_row, z_lhs, uz_row, sent, gram
):
    per_device = skel.shape[0]
    feats, count = qt.shape
    ph, pl_ = halves(pts[...] * scale)
    lhs[...] = jnp.concatenate([ph, pl_, ph, pl_], axis=1)
    qh, ql = halves(qt[...])
    u_row[...] = half_norm(qh, ql)
    both = jnp.concatenate([qh, ql], axis=0)
    for a in range(per_device):
        hot = pick(skel[a : a + 1, :], leaf_size).astype(F32).astype(BF16)
        z = dot(both[:, a * leaf_size : (a + 1) * leaf_size], hot).astype(BF16)
        zh, zl = z[:feats], z[feats:]
        z_lhs[a] = jnp.concatenate([zh, zl, zh, zl], axis=0)
        uz_row[a : a + 1, :] = half_norm(zh, zl)
    hot = pick(rskel[...], count).astype(F32).astype(BF16)
    r = dot(both, hot)
    r = r[:feats] + r[feats:]
    subs = sent.shape[0]
    sent[:, :count] = jnp.broadcast_to(cur[...], (subs, count))
    for f in range(feats // subs):
        sent[:, count + f * LANES : count + (f + 1) * LANES] = r[f * subs : (f + 1) * subs]
    g = dot(basis[...], basis[...], NT, HI)
    vecs = basis.shape[0]
    lane = lax.broadcasted_iota(jnp.int32, (vecs, LANES), 1)
    sub = lax.broadcasted_iota(jnp.int32, (vecs, LANES), 0)
    wide = dot(g, ((lane & (vecs - 1)) == sub).astype(F32), precision=HI)
    gram[...] = jnp.sum(jnp.where(lane // vecs == sub, wide, 0.0), axis=0, keepdims=True)


def weights(v, lm, rm):
    per_device, _, leaf_size = lm.shape
    root = None
    skel = []
    for a in range(per_device):
        piece = jnp.broadcast_to(v[:, a * leaf_size : (a + 1) * leaf_size], (8, leaf_size))
        skel.append(dot(piece, lm[a], NT, HI)[:1])
        part = dot(piece, rm[a], NT, HI)[:1]
        root = part if root is None else root + part
    return skel, root


def packed_vector(v, u_row, uz_row, lm, rm):
    skel, root = weights(v, lm, rm)
    scaled = [skel[a] * uz_row[a : a + 1, :] for a in range(len(skel))]
    return [v * u_row[...]] + scaled + [root]


def start_kernel(got, order, u_row, uz_row, lm, rm, skel, gram, v_row, sent):
    subs = got.shape[0]
    count = order.shape[1]
    tiles = count // LANES
    cur = jnp.concatenate([got[:, k * LANES : (k + 1) * LANES] for k in range(tiles)], axis=0)
    row, lane = split_order(order[...])
    hot = pick(row, subs * tiles).astype(F32).astype(BF16)
    picked = sum(dot(part, hot, TN) for part in thirds(cur))
    v = jnp.sum(jnp.where(pick(lane, LANES), picked, 0.0), axis=0, keepdims=True)
    v_row[...] = v
    sums = []
    for k in range(tiles):
        at = count + k * LANES
        sums.append(jnp.sum(got[:, at : at + LANES], axis=0, keepdims=True))
    skels = [skel[a : a + 1, :].astype(F32) for a in range(skel.shape[0])]
    block = jnp.concatenate(
        packed_vector(v, u_row, uz_row, lm, rm) + skels + sums + [gram[...]], axis=1
    )
    sent[...] = jnp.broadcast_to(block, sent.shape)


def apply_operator(
    info, window, lhs, z_lhs, u_row, uz_row, lm, rm, v_row, vec, tab, acc, far_acc, rhs
):
    per_device, skel_count, leaf_size = lm.shape
    subs, sides, feats, count = window.shape
    skel_at = count + per_device * skel_count
    tab_skel = skel_at + skel_count
    tab_root = tab_skel + per_device * skel_count
    leaf_count = vec.shape[0] // subs
    me = info[2 * per_device, 0]
    acc[...] = jnp.zeros_like(acc)
    far_acc[...] = jnp.zeros_like(far_acc)
    step_rows = 128

    def chunk(i, carry):
        side = i // subs
        dev = i % subs
        owner = (me + side + leaf_count - 1) % leaf_count
        rows = pl.ds(pl.multiple_of(owner * subs, subs), subs)

        def row_of(ref, at, size):
            block = ref[rows, at : at + size]
            mine = lax.broadcasted_iota(jnp.int32, block.shape, 0) == dev
            return jnp.sum(jnp.where(mine, block, 0.0), axis=0, keepdims=True)

        for j in range(per_device):
            slot = i * per_device + j
            qh, ql = halves(window[dev, side, :, j * leaf_size : (j + 1) * leaf_size])
            rhs[0 * feats : 1 * feats, :] = qh
            rhs[1 * feats : 2 * feats, :] = qh
            rhs[2 * feats : 3 * feats, :] = ql
            rhs[3 * feats : 4 * feats, :] = ql
            for a in range(per_device):

                @pl.when(info[a, slot] > 0)
                def near():
                    w = row_of(vec, j * leaf_size, leaf_size)
                    for r in range(leaf_size // step_rows):
                        at = a * leaf_size + r * step_rows
                        e = jnp.exp2(dot(lhs[at : at + step_rows, :], rhs[...]))
                        total = acc[at : at + step_rows, :]
                        for k in range(leaf_size // LANES):
                            part = slice(k * LANES, (k + 1) * LANES)
                            total = total + e[:, part] * w[:, part]
                        acc[at : at + step_rows, :] = total

            for a in range(per_device):

                @pl.when(info[per_device + a, slot] > 0)
                def far():
                    at = tab_skel + j * skel_count
                    index = row_of(tab, at, skel_count).astype(jnp.int32)
                    hot = pick(index, leaf_size).astype(F32).astype(BF16)
                    z = dot(rhs[feats : 3 * feats, :], hot).astype(BF16)
                    zh, zl = z[:feats], z[feats:]
                    z4 = jnp.concatenate([zh, zh, zl, zl], axis=0)
                    e = jnp.exp2(dot(z_lhs[a], z4, TN))
                    at = count + j * skel_count
                    w = row_of(vec, at, skel_count)
                    far_acc[a * skel_count : (a + 1) * skel_count, :] += e * w

        return carry

    lax.fori_loop(0, sides * subs, chunk, 0)

    def root_points(u):
        rows = pl.ds(pl.multiple_of(u * subs, subs), subs)
        r = jnp.concatenate(
            [
                tab[rows, tab_root + f * skel_count : tab_root + (f + 1) * skel_count]
                for f in range(feats // subs)
            ],
            axis=0,
        )
        return halves(r)

    rh, rl = root_points(me)
    r_lhs = jnp.concatenate([rh, rl, rh, rl], axis=0)
    own_norm = half_norm(rh, rl)

    def subtree(u, total):
        h, l = root_points(u)
        e = jnp.exp2(dot(r_lhs, jnp.concatenate([h, h, l, l], axis=0), TN))
        rows = pl.ds(pl.multiple_of(u * subs, subs), subs)
        w = jnp.sum(vec[rows, skel_at : skel_at + skel_count], axis=0, keepdims=True)
        w = jnp.where(u == me, 0.0, w * half_norm(h, l))
        return total + e * w

    top = lax.fori_loop(0, leaf_count, subtree, jnp.zeros((skel_count, skel_count), F32))
    root_out = jnp.broadcast_to(row_sums(top) * own_norm, (8, skel_count))
    outs = []
    for a in range(per_device):
        part = slice(a * leaf_size, (a + 1) * leaf_size)
        y = row_sums(acc[part, :]) * u_row[:, part]
        skel_out = row_sums(far_acc[a * skel_count : (a + 1) * skel_count, :]) * uz_row[a : a + 1, :]
        y = y + dot(jnp.broadcast_to(skel_out, (8, skel_count)), lm[a], precision=HI)[:1]
        y = y + dot(root_out, rm[a], precision=HI)[:1]
        outs.append(y + RIDGE * v_row[:, part])
    return jnp.concatenate(outs, axis=1)


def first_kernel(
    info, ritz, window, lhs, z_lhs, u_row, uz_row, lm, rm, v_row, vec, first_row, sent, acc, far_acc, rhs
):
    y = apply_operator(
        info, window, lhs, z_lhs, u_row, uz_row, lm, rm, v_row, vec, vec, acc, far_acc, rhs
    )
    first = v_row[...] - y / ritz[0]
    first_row[...] = first
    block = jnp.concatenate(packed_vector(first, u_row, uz_row, lm, rm), axis=1)
    sent[...] = jnp.broadcast_to(block, sent.shape)


def second_kernel(
    info, ritz, window, lhs, z_lhs, u_row, uz_row, lm, rm, v_row, vec, tab, tree_row, order, sent, acc, far_acc, rhs
):
    y = apply_operator(
        info, window, lhs, z_lhs, u_row, uz_row, lm, rm, v_row, vec, tab, acc, far_acc, rhs
    )
    grown = tree_row[...] - (v_row[...] - y / ritz[1])
    subs, count = sent.shape
    tiles = count // LANES
    row, lane = split_order(order[...])
    spread = jnp.where(pick(row, subs * tiles), grown, 0.0)
    hot = pick(lane, LANES).astype(F32).astype(BF16)
    placed = sum(dot(part, hot, NT) for part in thirds(spread))
    for k in range(tiles):
        sent[:, k * LANES : (k + 1) * LANES] = placed[k * subs : (k + 1) * subs]


def project_kernel(got, basis, user_row, sent):
    user = jnp.sum(got[...], axis=0, keepdims=True)
    user_row[...] = user
    b = basis[...]
    vecs = b.shape[0]
    proj = jnp.sum(b * user, axis=1, keepdims=True)
    norm = jnp.sum(user * user, axis=1, keepdims=True)
    lane = lax.broadcasted_iota(jnp.int32, (vecs, LANES), 1)
    sub = lax.broadcasted_iota(jnp.int32, (vecs, LANES), 0)
    row = jnp.sum(jnp.where(lane == sub, proj, 0.0), axis=0, keepdims=True)
    row = row + jnp.where(lane[:1] == vecs, norm, 0.0)
    sent[...] = jnp.broadcast_to(row, sent.shape)


def finish_kernel(got, tab, basis, user_row, orth, hess):
    b = basis[...]
    vecs = b.shape[0]
    total = jnp.sum(got[...], axis=0, keepdims=True)
    width = tab.shape[1]
    gram = jnp.sum(tab[:, width - LANES :], axis=0, keepdims=True)
    lane = lax.broadcasted_iota(jnp.int32, (vecs, LANES), 1)
    sub = lax.broadcasted_iota(jnp.int32, (vecs, LANES), 0)
    proj = jnp.sum(jnp.where(lane == sub, total, 0.0), axis=1, keepdims=True)
    left = jnp.sum(jnp.where(lane // vecs == sub, proj, 0.0), axis=0, keepdims=True)
    right = jnp.sum(jnp.where((lane & (vecs - 1)) == sub, proj, 0.0), axis=0, keepdims=True)
    one = lane[:1]
    norm = jnp.sum(jnp.where(one == vecs, total, 0.0), axis=1, keepdims=True)
    cross = jnp.sum(jnp.where(one < vecs, total * total, 0.0), axis=1, keepdims=True)
    quad = jnp.sum(left * right * gram, axis=1, keepdims=True)
    length = jnp.sqrt(jnp.maximum(norm - 2.0 * cross + quad, 0.0) + EPSILON)
    orth[...] = user_row[...] - jnp.sum(proj * b, axis=0, keepdims=True)
    hess[...] = jnp.where(one < vecs, total, jnp.broadcast_to(length, (1, LANES)))


def shards(
    points,
    leaf_maps,
    root_maps,
    current,
    krylov_basis,
    ritz_roots,
    point_order,
    skeleton,
    root_skeleton,
    near_list,
    far_list,
):
    per_device, skel_count, leaf_size = leaf_maps.shape
    count, feats = points.shape
    vecs = krylov_basis.shape[0]
    subs = lax.axis_size("sub")
    leaves = lax.axis_size("leaf")
    everyone = subs * leaves
    me = lax.axis_index("leaf")
    scale = math.sqrt(math.log2(math.e) / (feats / 2.0))
    qt = points.T * F32(scale)
    ring = [(i, (i + 1) % leaves) for i in range(leaves)]
    back = [(j, i) for i, j in ring]
    low = lax.ppermute(qt, "leaf", ring)
    high = lax.ppermute(qt, "leaf", back)
    window = lax.all_gather(jnp.stack([low, qt, high]), "sub", axis=0)

    sds = jax.ShapeDtypeStruct
    slots = jnp.arange(3 * subs * per_device, dtype=jnp.int32)
    near = jnp.any(near_list[:, :, None] == slots, axis=1).astype(jnp.int32)
    far = jnp.any(far_list[:, :, None] == slots, axis=1).astype(jnp.int32)
    info = jnp.concatenate([near, far, jnp.full((1, slots.shape[0]), me, jnp.int32)], axis=0)
    order = point_order.reshape(1, count)
    rskel = root_skeleton - lax.axis_index("sub") * count

    lhs, u_row, z_lhs, uz_row, sent, gram = call(
        functools.partial(prepare_kernel, scale, leaf_size),
        [
            sds((count, 4 * feats), BF16),
            sds((1, count), F32),
            sds((per_device, 4 * feats, skel_count), BF16),
            sds((per_device, skel_count), F32),
            sds((subs, count + (feats // subs) * skel_count), F32),
            sds((1, LANES), F32),
        ],
        points,
        qt,
        skeleton,
        rskel,
        current.reshape(1, count),
        krylov_basis,
        name="prepare",
    )
    got = lax.all_to_all(sent, "sub", 0, 0, tiled=True)
    vec_width = count + per_device * skel_count + skel_count
    tab_width = vec_width + per_device * skel_count + (feats // subs) * skel_count + LANES
    tree_row, sent = call(
        start_kernel,
        [sds((1, count), F32), sds((everyone, tab_width), F32)],
        got,
        order,
        u_row,
        uz_row,
        leaf_maps,
        root_maps,
        skeleton,
        gram,
        name="start",
    )
    tab = lax.all_to_all(sent, BOTH, 0, 0, tiled=True)
    scratch = [
        pltpu.VMEM((count, LANES), F32),
        pltpu.VMEM((per_device * skel_count, skel_count), F32),
        pltpu.VMEM((4 * feats, leaf_size), BF16),
    ]
    shared = (info, ritz_roots, window, lhs, z_lhs, u_row, uz_row, leaf_maps, root_maps)
    first_row, sent = call(
        first_kernel,
        [sds((1, count), F32), sds((everyone, vec_width), F32)],
        *shared,
        tree_row,
        tab,
        smem=(0, 1),
        scratch=scratch,
        name="first",
    )
    vec = lax.all_to_all(sent, BOTH, 0, 0, tiled=True)
    (sent,) = call(
        second_kernel,
        [sds((subs, count), F32)],
        *shared,
        first_row,
        vec,
        tab,
        tree_row,
        order,
        smem=(0, 1),
        scratch=scratch,
        name="second",
    )
    got = lax.all_to_all(sent, "sub", 0, 0, tiled=True)
    user_row, sent = call(
        project_kernel,
        [sds((1, count), F32), sds((everyone, LANES), F32)],
        got,
        krylov_basis,
        name="project",
    )
    got = lax.all_to_all(sent, BOTH, 0, 0, tiled=True)
    orth, hess = call(
        finish_kernel,
        [sds((1, count), F32), sds((1, LANES), F32)],
        got,
        tab,
        krylov_basis,
        user_row,
        name="finish",
    )
    return orth.reshape(count), hess[0, : vecs + 1]


def solution(mesh):
    return jax.shard_map(
        shards,
        mesh=mesh,
        in_specs=(
            P(("leaf", "sub"), None),
            P(("leaf", "sub"), None, None),
            P(("leaf", "sub"), None, None),
            P(("leaf", "sub")),
            P(None, ("leaf", "sub")),
            P(),
            P(("leaf", "sub")),
            P(("leaf", "sub"), None),
            P("leaf", None),
            P(("leaf", "sub"), None),
            P(("leaf", "sub"), None),
        ),
        out_specs=(P(("leaf", "sub")), P()),
        check_vma=False,
    )
```

time: 846 us -> 204 us (0.24)
  blocking collectives: 314 us -> 55.7 us
  local copies, waits for them, and re-layouts: 256 us -> 5.89 us
  matrix products: 226 us -> 0 us
  Pallas kernels: 0 us -> 71.3 us
  waiting for transfers between devices: 0.05 us -> 41.7 us
  other arithmetic: 17.4 us -> 2.23 us
    dot_general x80 -> x0, matrix products: 226 us -> none  [the longest x32 115 us: near_step(): jnp.einsum('bmf,bjnf->bjmn', own_points, sources, precision=HIGHEST_PREC)]
    gather x168 -> x0, local copies, waits for them, and re-layouts: 219 us -> none  [the longest x32 166 us: near_step(): sources = window_points[indices]]
    psum x4 -> x0, blocking collectives: 153 us -> none  [the longest x1 65.3 us: shards(): projections = lax.psum(local_proj, ('leaf', 'sub'))]
    all_gather x6 -> x0, blocking collectives: 134 us -> none  [the longest x2 67.4 us: operator(): root_weights = lax.all_gather(root_total[None], 'leaf', axis=0, tiled=True)]
    pallas_call x0 -> x6, Pallas kernels: none -> 71.3 us  [call(): pl.pallas_call(body, out_shape=outs, in_specs=specs, out_specs=[pl.BlockS...]
    all_to_all x0 -> x4, blocking collectives: none -> 55.7 us  [the longest x1 23 us: shards(): vec = lax.all_to_all(sent, BOTH, 0, 0, tiled=True)]
    unnamed x1 -> x0, blocking collectives: 26.8 us -> none
    all_to_all x0 -> x1, waiting for transfers between devices: none -> 25.3 us  [shards(): tab = lax.all_to_all(sent, BOTH, 0, 0, tiled=True)]
  transfers between devices with their start and end apart: 7 -> 4, of which waited for: 0 -> 4; matrix products, arithmetic and copies ran while one was open for 4% -> 2% of each run, Pallas kernels for 0% -> 1%
where the time goes in v1:
time: 204 us; the launch traced here: 203 us
  Pallas kernels  71.3 us (35%)
  blocking collectives  55.7 us (27%)
  waiting for transfers between devices  41.7 us (20%)
  between operations  14.2 us (7%)
  starting transfers between devices  12.3 us (6%)
  local copies, waits for them, and re-layouts  5.89 us (3%)
  other arithmetic  2.23 us (1%)
    pallas_call x6, Pallas kernels, call(): pl.pallas_call(body, out_shape=outs, in_specs=specs, out_specs=[pl.BlockS...  71.3 us
    all_to_all x1, waiting for transfers between devices, shards(): tab = lax.all_to_all(sent, BOTH, 0, 0, tiled=True)  25.3 us
    all_to_all x1, blocking collectives, shards(): vec = lax.all_to_all(sent, BOTH, 0, 0, tiled=True)  23 us
    all_to_all x2, blocking collectives, shards(): got = lax.all_to_all(sent, 'sub', 0, 0, tiled=True)  19.2 us
    all_to_all x1, blocking collectives, shards(): got = lax.all_to_all(sent, BOTH, 0, 0, tiled=True)  13.5 us
    ppermute x1, starting transfers between devices, shards(): high = lax.ppermute(qt, 'leaf', back)  6.85 us
    all_gather x1, waiting for transfers between devices, shards(): window = lax.all_gather(jnp.stack([low, qt, high]), 'sub', axis=0)  6.3 us
    all_to_all x1, starting transfers between devices, shards(): tab = lax.all_to_all(sent, BOTH, 0, 0, tiled=True)  5.38 us
  transfers between devices with their start and end apart: 4, of which 4 were waited for; matrix products, arithmetic and copies ran while one was open for 2% of the time, Pallas kernels for 1%

profile of v1, /device:TPU:1, one launch (start us, length us, event | category | flops | bytes accessed | tf_op | source)
XLA Modules:
  0.0 203.4 jit_solution(2811300450375013826)
XLA Ops:
  7.2 0.0 copy-start.7
  7.2 0.0 all-gather.3.cloned.1.call-start
  7.2 1.0 multiply_bitcast_fusion
  8.2 6.8 %collective-permute-start.1 = (f32[64,1024]{1,0:T(8,128)S(1)}, f32[64,1024]{1,0:T(8,128)S(1)}, u32[]{:S(2)}, u32[]{:S(2)}) collective-permute-start(f32[64,1024]{1,0:T(8,128)S(1)} %get-tuple-element.31.qt), channel_id=1, source_target_pairs={{8,0},{16,8},{24,16},{32,24},{40,32},{48,40},{56,48},{64,56},{72,6... | collective-permute-start | bytes 786440 | tf_op jit(solution)/shard_map/ppermute | solution.py:333
  15.1 0.0 collective-permute-start
  15.1 5.0 %collective-permute-done.1 = f32[64,1024]{1,0:T(8,128)S(1)} collective-permute-done((f32[64,1024]{1,0:T(8,128)S(1)}, f32[64,1024]{1,0:T(8,128)S(1)}, u32[]{:S(2)}, u32[]{:S(2)}) %collective-permute-start.1) | collective-permute-done | bytes 262176 | tf_op jit(solution)/shard_map/ppermute | solution.py:333
  20.1 5.2 %collective-permute-done = f32[64,1024]{1,0:T(8,128)S(1)} collective-permute-done((f32[64,1024]{1,0:T(8,128)S(1)}, f32[64,1024]{1,0:T(8,128)S(1)}, u32[]{:S(2)}, u32[]{:S(2)}) %collective-permute-start) | collective-permute-done | bytes 262176 | tf_op jit(solution)/shard_map/ppermute | solution.py:332
  25.3 0.9 pad_maximum_fusion
  26.2 0.0 all-gather.3.cloned.1.call-update
  26.3 0.2 copy.20.pts
  26.5 0.6 prepare.1
  27.1 0.1 copy.21
  27.2 11.0 %all_to_all.55 = f32[8,1,2048]{2,1,0:T(1,128)S(1)} all-to-all(f32[8,1,2048]{2,1,0:T(1,128)S(1)} %copy.21), channel_id=1, replica_groups=mesh['leaf'=16,'sub'=8] {'sub'}, dimensions={0} | all-to-all | bytes 131072 | tf_op jit(solution)/shard_map/all_to_all | solution.py:362
  38.2 1.3 start.1
  39.6 2.7 %copy.22 = f32[128,1,2816]{2,1,0:T(1,128)} copy(f32[128,1,2816]{2,0,1:T(8,128)S(1)} %bitcast.38) | data formatting | bytes 2883584 | tf_op jit(solution)/shard_map/all_to_all | solution.py:378
  42.2 5.4 %all-to-all-start.1 = ((f32[128,1,2816]{2,1,0:T(1,128)}), f32[128,1,2816]{2,1,0:T(1,128)}, u32[]{:S(2)}, u32[]{:S(2)}) async-start(f32[128,1,2816]{2,1,0:T(1,128)} %copy.22), calls=%async_computation.1 | async-start | bytes 2883584 | tf_op jit(solution)/shard_map/all_to_all | solution.py:378
  47.6 0.1 fusion
  47.8 0.1 fusion.1
  47.9 0.1 pad.5.clone
  47.9 0.1 add_add_fusion.info
  48.0 25.3 %all-to-all-done.1 = f32[128,1,2816]{2,1,0:T(1,128)} async-done(((f32[128,1,2816]{2,1,0:T(1,128)}), f32[128,1,2816]{2,1,0:T(1,128)}, u32[]{:S(2)}, u32[]{:S(2)}) %all-to-all-start.1) | async-done | bytes 1441824 | tf_op jit(solution)/shard_map/all_to_all | solution.py:378
  73.3 1.5 copy.34
  74.7 6.3 %all-gather.3.cloned.1.call-done = f32[24,64,1024]{2,1,0:T(8,128)} async-done(((f32[3,64,1024]{2,1,0:T(8,128)}), f32[24,64,1024]{2,1,0:T(8,128)}) %all-gather.3.cloned.1.call-update) | async-done | bytes 6291472 | tf_op jit(solution)/shard_map/all_gather | solution.py:334
  81.0 34.4 %first.1 = (f32[1,1024]{1,0:T(1,128)S(1)}, f32[128,1408]{1,0:T(8,128)S(1)}) custom-call(s32[5,48]{1,0:T(8,128)S(1)} %add_add_fusion.info, f32[2]{0:T(128)S(1)} %copy-done.6, f32[8,3,64,1024]{3,2,1,0:T(8,128)} %bitcast.49, bf16[1024,256]{1,0:T(8,128)(2,1)S(1)} %get-tuple-element.16.lhs, bf16[2,256,128]{2,1,0:T(8,128)(2,1)S(1)} %get-tuple-element.17.z_lhs, ...), custom_call_target="tpu_custom_call" | custom-call | tf_op jit(solution)/shard_map/first/pallas_call | solution.py:62
  115.5 0.7 copy.23
  116.2 23.0 %all_to_all.56 = f32[128,1,1408]{2,1,0:T(1,128)S(1)} all-to-all(f32[128,1,1408]{2,1,0:T(1,128)S(1)} %copy.23), channel_id=1, replica_groups=mesh['leaf'=16,'sub'=8] {'leaf','sub'}, dimensions={0} | all-to-all | bytes 1441792 | tf_op jit(solution)/shard_map/all_to_all | solution.py:395
  139.3 34.2 %second.1 = f32[8,1024]{1,0:T(8,128)S(1)} custom-call(s32[5,48]{1,0:T(8,128)S(1)} %add_add_fusion.info, f32[2]{0:T(128)S(1)} %copy-done.6, f32[8,3,64,1024]{3,2,1,0:T(8,128)} %bitcast.50, bf16[1024,256]{1,0:T(8,128)(2,1)S(1)} %get-tuple-element.16.lhs, bf16[2,256,128]{2,1,0:T(8,128)(2,1)S(1)} %get-tuple-element.17.z_lhs, ...), custom_call_target="tpu_custom_call" | custom-call | tf_op jit(solution)/shard_map/second/pallas_call | solution.py:62
  173.5 8.2 %all_to_all.57 = f32[8,1,1024]{2,1,0:T(1,128)S(1)} all-to-all(f32[8,1,1024]{2,1,0:T(1,128)S(1)} %copy.24), channel_id=1, replica_groups=mesh['leaf'=16,'sub'=8] {'sub'}, dimensions={0} | all-to-all | bytes 65536 | tf_op jit(solution)/shard_map/all_to_all | solution.py:409
  181.8 0.1 project.1
  181.9 13.5 %all_to_all.58 = f32[128,1,128]{2,1,0:T(1,128)S(1)} all-to-all(f32[128,1,128]{2,1,0:T(1,128)S(1)} %bitcast.45), channel_id=1, replica_groups=mesh['leaf'=16,'sub'=8] {'leaf','sub'}, dimensions={0} | all-to-all | bytes 131072 | tf_op jit(solution)/shard_map/all_to_all | solution.py:417
  195.3 0.7 finish.1
  196.1 0.5 slice_bitcast_fusion
  (28 shorter events, 0.2 us)
Async XLA Ops:
  7.2 19.1 %copy-start.7 = (f32[1024,64]{0,1:T(8,128)S(1)}, f32[1024,64]{0,1:T(8,128)}, u32[]{:S(2)}) copy-start(f32[1024,64]{0,1:T(8,128)} %param.11) | copy-start | bytes 786436
  7.2 73.9 %all-gather.3.cloned.1.call-start = ((), (), s32[]{:S(2)}) async-start(), calls=%async_computation.5 | async-start | bytes 7077888 | tf_op jit(solution)/shard_map/all_gather | solution.py:334
  8.2 11.8 %collective-permute-start.1 = (f32[64,1024]{1,0:T(8,128)S(1)}, f32[64,1024]{1,0:T(8,128)S(1)}, u32[]{:S(2)}, u32[]{:S(2)}) collective-permute-start(f32[64,1024]{1,0:T(8,128)S(1)} %get-tuple-element.31.qt), channel_id=1, source_target_pairs={{8,0},{16,8},{24,16},{32,24},{40,32},{48,40},{56,48},{64,56},{72,6... | collective-permute-start | bytes 786440 | tf_op jit(solution)/shard_map/ppermute | solution.py:333
  15.1 10.2 %collective-permute-start = (f32[64,1024]{1,0:T(8,128)S(1)}, f32[64,1024]{1,0:T(8,128)S(1)}, u32[]{:S(2)}, u32[]{:S(2)}) collective-permute-start(f32[64,1024]{1,0:T(8,128)S(1)} %get-tuple-element.31.qt), channel_id=1, source_target_pairs={{0,8},{8,16},{16,24},{24,32},{32,40},{40,48},{48,56},{56,64},{64,7... | collective-permute-start | bytes 786440 | tf_op jit(solution)/shard_map/ppermute | solution.py:332
  25.3 1.2 copy-start.10
  25.3 1.2 copy-start.2
  25.3 1.2 copy-start.4
  25.3 1.2 copy-start.5
  26.2 12.0 %copy-start = (f32[2,128,512]{2,1,0:T(8,128)S(1)}, f32[2,128,512]{2,1,0:T(8,128)}, u32[]{:S(2)}) copy-start(f32[2,128,512]{2,1,0:T(8,128)} %lm.5) | copy-start | bytes 1572868
  26.2 12.0 %copy-start.1 = (f32[2,128,512]{2,1,0:T(8,128)S(1)}, f32[2,128,512]{2,1,0:T(8,128)}, u32[]{:S(2)}) copy-start(f32[2,128,512]{2,1,0:T(8,128)} %rm.5) | copy-start | bytes 1572868
  26.2 12.0 %copy-start.3 = (s32[1024]{0:T(1024)S(1)}, s32[1024]{0:T(1024)}, u32[]{:S(2)}) copy-start(s32[1024]{0:T(1024)} %param.17) | copy-start | bytes 12292
  42.2 5.4 %copy-start.8 = (s32[2,32]{1,0:T(2,128)S(1)}, s32[2,32]{1,0:T(2,128)}, u32[]{:S(2)}) copy-start(s32[2,32]{1,0:T(2,128)} %param.20) | copy-start | bytes 772
  42.2 5.5 %copy-start.9 = (s32[2,4]{1,0:T(2,128)S(1)}, s32[2,4]{1,0:T(2,128)}, u32[]{:S(2)}) copy-start(s32[2,4]{1,0:T(2,128)} %param.21) | copy-start | bytes 100
  42.2 31.0 %all-to-all-start.1 = ((f32[128,1,2816]{2,1,0:T(1,128)}), f32[128,1,2816]{2,1,0:T(1,128)}, u32[]{:S(2)}, u32[]{:S(2)}) async-start(f32[128,1,2816]{2,1,0:T(1,128)} %copy.22), calls=%async_computation.1 | async-start | bytes 2883584 | tf_op jit(solution)/shard_map/all_to_all | solution.py:378
  48.0 33.0 %copy-start.6 = (f32[2]{0:T(128)S(1)}, f32[2]{0:T(128)}, u32[]{:S(2)}) copy-start(f32[2]{0:T(128)} %ritz.3) | copy-start | bytes 28
Sparse Core Ops, SparseCore 0:
  26.4 54.6 all-gather.2

commit v2 on v1

v2 whole, which is shorter than its diff:
```python
import functools
import math

import jax
import jax.numpy as jnp
from jax import lax
from jax.experimental import pallas as pl
from jax.experimental.pallas import tpu as pltpu
from jax.sharding import PartitionSpec as P

F32 = jnp.float32
BF16 = jnp.bfloat16
HI = lax.Precision.HIGHEST
RIDGE = 1.0
EPSILON = 1e-06
LANES = 128
BOTH = ("leaf", "sub")
STEP = 256
UNROLL = 8
VMEM_LIMIT = 50 * 1024 * 1024
NT = (((1,), (1,)), ((), ()))
TN = (((0,), (0,)), ((), ()))


def dot(a, b, dims=(((1,), (0,)), ((), ())), precision=None):
    return lax.dot_general(a, b, dims, precision=precision, preferred_element_type=F32)


def halves(x):
    h = x.astype(BF16)
    return h, (x - h.astype(F32)).astype(BF16)


def thirds(x):
    a = x.astype(BF16)
    r = x - a.astype(F32)
    b = r.astype(BF16)
    return a, b, (r - b.astype(F32)).astype(BF16)


def row_sums(block):
    return jnp.sum(block.T, axis=0, keepdims=True)


def fold(wide):
    return sum(wide[:, at : at + LANES] for at in range(0, wide.shape[1], LANES))


def half_norm(h, l):
    x = h.astype(F32) + l.astype(F32)
    return jnp.exp2(-0.5 * jnp.sum(x * x, axis=0, keepdims=True))


def pick(index_row, count):
    shape = (count, index_row.shape[1])
    return lax.broadcasted_iota(jnp.int32, shape, 0) == jnp.broadcast_to(index_row, shape)


def split_order(order):
    row = (lax.shift_right_logical(order, 7) & 7) * 8 + lax.shift_right_logical(order, 10)
    return row, order & 127


def call(body, outs, *args, smem=(), far=(), scratch=(), cost=None, name=None):
    places = [pltpu.SMEM if i in smem else pl.ANY if i in far else pltpu.VMEM for i in range(len(args))]
    specs = [pl.BlockSpec(memory_space=place) for place in places]
    return pl.pallas_call(
        body,
        out_shape=outs,
        in_specs=specs,
        out_specs=[pl.BlockSpec(memory_space=pltpu.VMEM)] * len(outs),
        scratch_shapes=list(scratch),
        compiler_params=pltpu.CompilerParams(vmem_limit_bytes=VMEM_LIMIT),
        cost_estimate=cost,
        name=name,
    )(*args)


def prepare_kernel(
    scale, leaf_size, pts, qt, skel, rskel, cur, basis, lhs, u_row, z_lhs, uz_row, uz_col, sent, gram
):
    per_device, skel_count = skel.shape
    feats, count = qt.shape
    ph, pl_ = halves(pts[...] * scale)
    lhs[...] = jnp.concatenate([ph, pl_, ph, pl_], axis=1)
    qh, ql = halves(qt[...])
    u_row[...] = half_norm(qh, ql)
    both = jnp.concatenate([qh, ql], axis=0)
    for a in range(per_device):
        hot = pick(skel[a : a + 1, :], leaf_size).astype(F32).astype(BF16)
        z = dot(both[:, a * leaf_size : (a + 1) * leaf_size], hot)
        zh, zl = z[:feats].astype(BF16), z[feats:].astype(BF16)
        uz_row[a : a + 1, :] = half_norm(zh, zl)
        turned = z.T
        out = slice(a * skel_count, (a + 1) * skel_count)
        z_lhs[out, :] = jnp.concatenate([turned, turned], axis=1).astype(BF16)
        whole = turned[:, :feats] + turned[:, feats:]
        norm = jnp.exp2(-0.5 * jnp.sum(whole * whole, axis=1, keepdims=True))
        uz_col[out, :] = jnp.broadcast_to(norm, (skel_count, LANES))
    hot = pick(rskel[...], count).astype(F32).astype(BF16)
    r = dot(both, hot)
    r = r[:feats] + r[feats:]
    subs = sent.shape[0]
    sent[:, :count] = jnp.broadcast_to(cur[...], (subs, count))
    for f in range(feats // subs):
        sent[:, count + f * LANES : count + (f + 1) * LANES] = r[f * subs : (f + 1) * subs]
    g = dot(basis[...], basis[...], NT, HI)
    vecs = basis.shape[0]
    lane = lax.broadcasted_iota(jnp.int32, (vecs, LANES), 1)
    sub = lax.broadcasted_iota(jnp.int32, (vecs, LANES), 0)
    wide = dot(g, ((lane & (vecs - 1)) == sub).astype(F32), precision=HI)
    gram[...] = jnp.sum(jnp.where(lane // vecs == sub, wide, 0.0), axis=0, keepdims=True)


def packed_vector(v, u_row, uz_row, lm, rm):
    per_device, _, leaf_size = lm.shape
    root = None
    skel = []
    for a in range(per_device):
        piece = v[:, a * leaf_size : (a + 1) * leaf_size]
        skel.append(row_sums(fold(lm[a] * piece)) * uz_row[a : a + 1, :])
        part = fold(rm[a] * piece)
        root = part if root is None else root + part
    return [v * u_row[...]] + skel + [row_sums(root)]


def start_kernel(got, order, u_row, uz_row, lm, rm, skel, gram, v_row, sent):
    subs = got.shape[0]
    count = order.shape[1]
    tiles = count // LANES
    cur = jnp.concatenate([got[:, k * LANES : (k + 1) * LANES] for k in range(tiles)], axis=0)
    row, lane = split_order(order[...])
    hot = pick(row, subs * tiles).astype(F32).astype(BF16)
    picked = sum(dot(part, hot, TN) for part in thirds(cur))
    v = jnp.sum(jnp.where(pick(lane, LANES), picked, 0.0), axis=0, keepdims=True)
    v_row[...] = v
    sums = []
    for k in range(tiles):
        at = count + k * LANES
        sums.append(jnp.sum(got[:, at : at + LANES], axis=0, keepdims=True))
    skels = [skel[a : a + 1, :].astype(F32) for a in range(skel.shape[0])]
    block = jnp.concatenate(
        packed_vector(v, u_row, uz_row, lm, rm) + skels + sums + [gram[...]], axis=1
    )
    sent[...] = jnp.broadcast_to(block, sent.shape)


def top_kernel(feats, info, tab, blocks):
    leaf_count, skel_count, _ = blocks.shape
    subs = tab.shape[0] // leaf_count
    at = tab.shape[1] - LANES - feats // subs * skel_count
    me = info[info.shape[0] - 1, 0]

    def root_points(u):
        rows = pl.ds(pl.multiple_of(u * subs, subs), subs)
        tiles = [tab[rows, at + f * skel_count : at + (f + 1) * skel_count] for f in range(feats // subs)]
        return jnp.concatenate(tiles, axis=0)

    turned = root_points(me).T
    th, tl = halves(turned)
    left = jnp.concatenate([th, tl, th, tl], axis=1)
    whole = th.astype(F32) + tl.astype(F32)
    own = jnp.exp2(-0.5 * jnp.sum(whole * whole, axis=1, keepdims=True))

    def subtree(u, carry):
        h, l = halves(root_points(u))
        e = jnp.exp2(dot(left, jnp.concatenate([h, h, l, l], axis=0)))
        side = jnp.where(u == me, 0.0, half_norm(h, l))
        blocks[u] = e * side * own
        return carry

    lax.fori_loop(0, leaf_count, subtree, 0, unroll=2)


def owners(info, leaf_count, sides):
    me = info[info.shape[0] - 1, 0]
    return [(me + side + leaf_count - 1) % leaf_count for side in range(sides)]


def spread_values(info, vec, values, subs, leaf_size):
    slots = values.shape[0]
    leaf_count = vec.shape[0] // subs
    per_side = slots // 3
    for side, owner in enumerate(owners(info, leaf_count, 3)):
        block = vec[pl.ds(pl.multiple_of(owner * subs, subs), subs), : per_side // subs * leaf_size]
        for n in range(per_side):
            dev, j = n // (per_side // subs), n % (per_side // subs)
            row = block[dev : dev + 1, j * leaf_size : (j + 1) * leaf_size]
            values[side * per_side + n] = jnp.broadcast_to(row, (8, leaf_size))


def picked_row(ref, info, slot, per_side, subs, offset, size):
    leaf_count = ref.shape[0] // subs
    me = info[info.shape[0] - 1, 0]
    per_device = per_side // subs
    side, n = slot // per_side, slot % per_side
    owner = (me + side + leaf_count - 1) % leaf_count
    rows = pl.ds(pl.multiple_of(owner * subs, subs), subs)
    block = ref[rows, offset : offset + per_device * size]
    sub = lax.broadcasted_iota(jnp.int32, (subs, size), 0)
    out = jnp.zeros((1, size), F32)
    for j in range(per_device):
        mine = (sub == n // per_device) & (n % per_device == j)
        part = block[:, j * size : (j + 1) * size]
        out = out + jnp.sum(jnp.where(mine, part, 0.0), axis=0, keepdims=True)
    return out


def quad(pair):
    feats = pair.shape[0] // 2
    h, l = pair[:feats, :], pair[feats:, :]
    return jnp.concatenate([h, h, l, l], axis=0)


def near_sums(info, split, values, lhs, acc, near_count):
    per_device = (info.shape[0] - 1) // 2
    leaf_size = split.shape[2]
    acc[...] = jnp.zeros_like(acc)
    step = STEP

    def visit(n, carry):
        for a in range(per_device):
            slot = info[a, n]
            right = quad(split[slot])
            w = values[slot]
            for r in range(leaf_size // step):
                at = a * leaf_size + r * step
                e = jnp.exp2(dot(lhs[at : at + step, :], right))
                e = e.reshape(step // 8, 8, leaf_size) * w[None]
                acc[at : at + step, :] += fold(e.reshape(step, leaf_size))
        return carry

    lax.fori_loop(0, near_count, visit, 0, unroll=UNROLL)


def far_sums(info, far_blocks, vec, far_count, subs, per_side, offset):
    per_device = (info.shape[0] - 1) // 2
    skel_count = far_blocks.shape[1]
    outs = []
    for a in range(per_device):
        total = jnp.zeros((skel_count, LANES), F32)
        for n in range(far_count):
            slot = info[per_device + a, n]
            w = picked_row(vec, info, slot, per_side, subs, offset, skel_count)
            total = total + far_blocks[a * far_count + n] * w
        outs.append(jnp.sum(total, axis=1, keepdims=True))
    return outs


def top_sums(top, vec, subs, offset):
    leaf_count, skel_count, _ = top.shape
    total = jnp.zeros((skel_count, LANES), F32)
    for u in range(leaf_count):
        w = jnp.sum(vec[u * subs : (u + 1) * subs, offset : offset + skel_count], axis=0, keepdims=True)
        total = total + top[u] * w
    return jnp.sum(total, axis=1, keepdims=True)


def gathered(acc, u_row, uz_col, lm, rm, v_row, skel_out, root_out):
    per_device, skel_count, leaf_size = lm.shape
    outs = []
    for a in range(per_device):
        part = slice(a * leaf_size, (a + 1) * leaf_size)
        y = row_sums(acc[part, :]) * u_row[:, part]
        col = skel_out[a] * uz_col[a * skel_count : (a + 1) * skel_count, :1]
        y = y + jnp.sum(lm[a] * col + rm[a] * root_out, axis=0, keepdims=True)
        outs.append(y + RIDGE * v_row[:, part])
    return jnp.concatenate(outs, axis=1)


def first_kernel(
    counts, info, ritz, window, lhs, z_lhs, u_row, uz_row, uz_col, lm, rm, top, v_row, vec,
    first_row, sent, split, far_blocks, landed, values, acc, sems,
):
    near_count, far_count = counts
    per_device, skel_count, leaf_size = lm.shape
    subs, sides, feats, count = window.shape
    per_side = subs * per_device
    copies = [pltpu.make_async_copy(window.at[d], landed.at[d], sems.at[d]) for d in range(subs)]
    for copy in copies:
        copy.start()
    spread_values(info, vec, values, subs, leaf_size)
    skel_at = count + per_device * skel_count
    root_out = top_sums(top, vec, subs, skel_at)
    for d in range(subs):
        copies[d].wait()
        for side in range(sides):
            for j in range(per_device):
                h, l = halves(landed[d, side, :, j * leaf_size : (j + 1) * leaf_size])
                slot = side * per_side + d * per_device + j
                split[slot, :feats, :] = h
                split[slot, feats:, :] = l
    near_sums(info, split, values, lhs, acc, near_count)
    index_at = skel_at + skel_count
    for a in range(per_device):
        for n in range(far_count):
            slot = info[per_device + a, n]
            index = picked_row(vec, info, slot, per_side, subs, index_at, skel_count).astype(jnp.int32)
            hot = pick(index, leaf_size).astype(F32).astype(BF16)
            z = dot(split[slot], hot).astype(BF16)
            left = z_lhs[a * skel_count : (a + 1) * skel_count, :]
            far_blocks[a * far_count + n] = jnp.exp2(dot(left, quad(z)))
    skel_out = far_sums(info, far_blocks, vec, far_count, subs, per_side, count)
    y = gathered(acc, u_row, uz_col, lm, rm, v_row, skel_out, root_out)
    first = v_row[...] - y / ritz[0]
    first_row[...] = first
    block = jnp.concatenate(packed_vector(first, u_row, uz_row, lm, rm), axis=1)
    sent[...] = jnp.broadcast_to(block, sent.shape)


def second_kernel(
    counts, info, ritz, lhs, u_row, uz_col, lm, rm, top, split, far_blocks, v_row, vec, tree_row, order,
    sent, values, acc,
):
    near_count, far_count = counts
    per_device, skel_count, leaf_size = lm.shape
    subs, count = sent.shape
    spread_values(info, vec, values, subs, leaf_size)
    root_out = top_sums(top, vec, subs, count + per_device * skel_count)
    skel_out = far_sums(info, far_blocks, vec, far_count, subs, subs * per_device, count)
    near_sums(info, split, values, lhs, acc, near_count)
    y = gathered(acc, u_row, uz_col, lm, rm, v_row, skel_out, root_out)
    grown = tree_row[...] - (v_row[...] - y / ritz[1])
    tiles = count // LANES
    row, lane = split_order(order[...])
    spread = jnp.where(pick(row, subs * tiles), grown, 0.0)
    hot = pick(lane, LANES).astype(F32).astype(BF16)
    placed = sum(dot(part, hot, NT) for part in thirds(spread))
    for k in range(tiles):
        sent[:, k * LANES : (k + 1) * LANES] = placed[k * subs : (k + 1) * subs]


def project_kernel(got, basis, user_row, sent):
    user = jnp.sum(got[...], axis=0, keepdims=True)
    user_row[...] = user
    b = basis[...]
    vecs = b.shape[0]
    proj = jnp.sum(b * user, axis=1, keepdims=True)
    norm = jnp.sum(user * user, axis=1, keepdims=True)
    lane = lax.broadcasted_iota(jnp.int32, (vecs, LANES), 1)
    sub = lax.broadcasted_iota(jnp.int32, (vecs, LANES), 0)
    row = jnp.sum(jnp.where(lane == sub, proj, 0.0), axis=0, keepdims=True)
    row = row + jnp.where(lane[:1] == vecs, norm, 0.0)
    sent[...] = jnp.broadcast_to(row, sent.shape)


def finish_kernel(got, tab, basis, user_row, orth, hess):
    b = basis[...]
    vecs = b.shape[0]
    total = jnp.sum(got[...], axis=0, keepdims=True)
    width = tab.shape[1]
    gram = jnp.sum(tab[:, width - LANES :], axis=0, keepdims=True)
    lane = lax.broadcasted_iota(jnp.int32, (vecs, LANES), 1)
    sub = lax.broadcasted_iota(jnp.int32, (vecs, LANES), 0)
    proj = jnp.sum(jnp.where(lane == sub, total, 0.0), axis=1, keepdims=True)
    left = jnp.sum(jnp.where(lane // vecs == sub, proj, 0.0), axis=0, keepdims=True)
    right = jnp.sum(jnp.where((lane & (vecs - 1)) == sub, proj, 0.0), axis=0, keepdims=True)
    one = lane[:1]
    norm = jnp.sum(jnp.where(one == vecs, total, 0.0), axis=1, keepdims=True)
    cross = jnp.sum(jnp.where(one < vecs, total * total, 0.0), axis=1, keepdims=True)
    quad = jnp.sum(left * right * gram, axis=1, keepdims=True)
    length = jnp.sqrt(jnp.maximum(norm - 2.0 * cross + quad, 0.0) + EPSILON)
    orth[...] = user_row[...] - jnp.sum(proj * b, axis=0, keepdims=True)
    hess[...] = jnp.where(one < vecs, total, jnp.broadcast_to(length, (1, LANES)))


def shards(
    points,
    leaf_maps,
    root_maps,
    current,
    krylov_basis,
    ritz_roots,
    point_order,
    skeleton,
    root_skeleton,
    near_list,
    far_list,
):
    per_device, skel_count, leaf_size = leaf_maps.shape
    count, feats = points.shape
    vecs = krylov_basis.shape[0]
    subs = lax.axis_size("sub")
    leaves = lax.axis_size("leaf")
    everyone = subs * leaves
    me = lax.axis_index("leaf")
    scale = math.sqrt(math.log2(math.e) / (feats / 2.0))
    qt = points.T * F32(scale)
    ring = [(i, (i + 1) % leaves) for i in range(leaves)]
    back = [(j, i) for i, j in ring]
    low = lax.ppermute(qt, "leaf", ring)
    high = lax.ppermute(qt, "leaf", back)
    window = lax.all_gather(jnp.stack([low, qt, high]), "sub", axis=0)

    sds = jax.ShapeDtypeStruct
    near_count, far_count = near_list.shape[1], far_list.shape[1]
    info = jnp.concatenate(
        [
            near_list,
            jnp.pad(far_list, ((0, 0), (0, near_count - far_count))),
            jnp.full((1, near_count), me, jnp.int32),
        ],
        axis=0,
    )
    order = point_order.reshape(1, count)
    rskel = root_skeleton - lax.axis_index("sub") * count

    lhs, u_row, z_lhs, uz_row, uz_col, sent, gram = call(
        functools.partial(prepare_kernel, scale, leaf_size),
        [
            sds((count, 4 * feats), BF16),
            sds((1, count), F32),
            sds((per_device * skel_count, 4 * feats), BF16),
            sds((per_device, skel_count), F32),
            sds((per_device * skel_count, LANES), F32),
            sds((subs, count + (feats // subs) * skel_count), F32),
            sds((1, LANES), F32),
        ],
        points,
        qt,
        skeleton,
        rskel,
        current.reshape(1, count),
        krylov_basis,
        name="prepare",
    )
    got = lax.all_to_all(sent, "sub", 0, 0, tiled=True)
    vec_width = count + per_device * skel_count + skel_count
    tab_width = vec_width + per_device * skel_count + (feats // subs) * skel_count + LANES
    tree_row, sent = call(
        start_kernel,
        [sds((1, count), F32), sds((everyone, tab_width), F32)],
        got,
        order,
        u_row,
        uz_row,
        leaf_maps,
        root_maps,
        skeleton,
        gram,
        name="start",
    )
    tab = lax.all_to_all(sent, BOTH, 0, 0, tiled=True)
    (top,) = call(
        functools.partial(top_kernel, feats),
        [sds((leaves, skel_count, skel_count), F32)],
        info,
        tab,
        smem=(0,),
        name="top",
    )
    slots = 3 * subs * per_device
    counts = (near_count, far_count)
    spread = pltpu.VMEM((slots, 8, leaf_size), F32)
    sums = pltpu.VMEM((count, LANES), F32)
    first_row, sent, split, far_blocks = call(
        functools.partial(first_kernel, counts),
        [
            sds((1, count), F32),
            sds((everyone, vec_width), F32),
            sds((slots, 2 * feats, leaf_size), BF16),
            sds((per_device * far_count, skel_count, skel_count), F32),
        ],
        info,
        ritz_roots,
        window,
        lhs,
        z_lhs,
        u_row,
        uz_row,
        uz_col,
        leaf_maps,
        root_maps,
        top,
        tree_row,
        tab,
        smem=(0, 1),
        far=(2,),
        scratch=[pltpu.VMEM(window.shape, F32), spread, sums, pltpu.SemaphoreType.DMA((subs,))],
        name="first",
    )
    vec = lax.all_to_all(sent, BOTH, 0, 0, tiled=True)
    (sent,) = call(
        functools.partial(second_kernel, counts),
        [sds((subs, count), F32)],
        info,
        ritz_roots,
        lhs,
        u_row,
        uz_col,
        leaf_maps,
        root_maps,
        top,
        split,
        far_blocks,
        first_row,
        vec,
        tree_row,
        order,
        smem=(0, 1),
        scratch=[spread, sums],
        name="second",
    )
    got = lax.all_to_all(sent, "sub", 0, 0, tiled=True)
    user_row, sent = call(
        project_kernel,
        [sds((1, count), F32), sds((everyone, LANES), F32)],
        got,
        krylov_basis,
        name="project",
    )
    got = lax.all_to_all(sent, BOTH, 0, 0, tiled=True)
    orth, hess = call(
        finish_kernel,
        [sds((1, count), F32), sds((1, LANES), F32)],
        got,
        tab,
        krylov_basis,
        user_row,
        name="finish",
    )
    return orth.reshape(count), hess[0, : vecs + 1]


def solution(mesh):
    return jax.shard_map(
        shards,
        mesh=mesh,
        in_specs=(
            P(("leaf", "sub"), None),
            P(("leaf", "sub"), None, None),
            P(("leaf", "sub"), None, None),
            P(("leaf", "sub")),
            P(None, ("leaf", "sub")),
            P(),
            P(("leaf", "sub")),
            P(("leaf", "sub"), None),
            P("leaf", None),
            P(("leaf", "sub"), None),
            P(("leaf", "sub"), None),
        ),
        out_specs=(P(("leaf", "sub")), P()),
        check_vma=False,
    )
```

time: 204 us -> 167 us (0.82)
  Pallas kernels: 71.3 us -> 36.5 us
  waiting for transfers between devices: 41.7 us -> 39.3 us
    pallas_call x6 -> x7, Pallas kernels: 71.3 us -> 36.5 us  [call(): pl.pallas_call(body, out_shape=outs, in_specs=specs, out_specs=[pl.BlockS...]
    all_gather x1, waiting for transfers between devices: 6.3 us -> 3.63 us  [shards(): window = lax.all_gather(jnp.stack([low, qt, high]), 'sub', axis=0)]
  transfers between devices with their start and end apart: 4 -> 4, of which waited for: 4 -> 4; matrix products, arithmetic and copies ran while one was open for 2% -> 3% of each run, Pallas kernels for 1% -> 2%
where the time goes in v2:
time: 167 us
  blocking collectives  55.7 us (33%)
  waiting for transfers between devices  39.3 us (24%)
  Pallas kernels  36.5 us (22%)
  between operations  14.3 us (9%)
  starting transfers between devices  12.3 us (7%)
  local copies, waits for them, and re-layouts  6.86 us (4%)
  other arithmetic  2.03 us (1%)
    pallas_call x7, Pallas kernels, call(): pl.pallas_call(body, out_shape=outs, in_specs=specs, out_specs=[pl.BlockS...  36.5 us
    all_to_all x1, waiting for transfers between devices, shards(): tab = lax.all_to_all(sent, BOTH, 0, 0, tiled=True)  25.5 us
    all_to_all x1, blocking collectives, shards(): vec = lax.all_to_all(sent, BOTH, 0, 0, tiled=True)  23 us
    all_to_all x2, blocking collectives, shards(): got = lax.all_to_all(sent, 'sub', 0, 0, tiled=True)  19.2 us
    all_to_all x1, blocking collectives, shards(): got = lax.all_to_all(sent, BOTH, 0, 0, tiled=True)  13.5 us
    ppermute x1, starting transfers between devices, shards(): high = lax.ppermute(qt, 'leaf', back)  6.85 us
    all_to_all x1, starting transfers between devices, shards(): tab = lax.all_to_all(sent, BOTH, 0, 0, tiled=True)  5.37 us
    ppermute x1, waiting for transfers between devices, shards(): low = lax.ppermute(qt, 'leaf', ring)  5.2 us
  transfers between devices with their start and end apart: 4, of which 4 were waited for; matrix products, arithmetic and copies ran while one was open for 3% of the time, Pallas kernels for 2%

profile of v2, /device:TPU:1, one launch (start us, length us, event | category | flops | bytes accessed | tf_op | source)
XLA Modules:
  0.0 166.9 jit_solution(9062986363243323046)
XLA Ops:
  7.2 0.0 all-gather.3.cloned.1.call-start
  7.2 1.0 multiply_bitcast_fusion
  8.2 6.8 %collective-permute-start.1 = (f32[64,1024]{1,0:T(8,128)S(1)}, f32[64,1024]{1,0:T(8,128)S(1)}, u32[]{:S(2)}, u32[]{:S(2)}) collective-permute-start(f32[64,1024]{1,0:T(8,128)S(1)} %get-tuple-element.37.qt), channel_id=1, source_target_pairs={{8,0},{16,8},{24,16},{32,24},{40,32},{48,40},{56,48},{64,56},{72,6... | collective-permute-start | bytes 786440 | tf_op jit(solution)/shard_map/ppermute | solution.py:392
  15.1 0.0 collective-permute-start
  15.1 5.0 %collective-permute-done.1 = f32[64,1024]{1,0:T(8,128)S(1)} collective-permute-done((f32[64,1024]{1,0:T(8,128)S(1)}, f32[64,1024]{1,0:T(8,128)S(1)}, u32[]{:S(2)}, u32[]{:S(2)}) %collective-permute-start.1) | collective-permute-done | bytes 262176 | tf_op jit(solution)/shard_map/ppermute | solution.py:392
  20.1 5.2 %collective-permute-done = f32[64,1024]{1,0:T(8,128)S(1)} collective-permute-done((f32[64,1024]{1,0:T(8,128)S(1)}, f32[64,1024]{1,0:T(8,128)S(1)}, u32[]{:S(2)}, u32[]{:S(2)}) %collective-permute-start) | collective-permute-done | bytes 262176 | tf_op jit(solution)/shard_map/ppermute | solution.py:391
  25.3 0.9 pad_maximum_fusion
  26.2 0.0 all-gather.3.cloned.1.call-update
  26.3 0.2 copy.14.pts
  26.5 0.6 prepare.1
  27.2 0.1 copy.15
  27.2 11.0 %all_to_all.55 = f32[8,1,2048]{2,1,0:T(1,128)S(1)} all-to-all(f32[8,1,2048]{2,1,0:T(1,128)S(1)} %copy.15), channel_id=1, replica_groups=mesh['leaf'=16,'sub'=8] {'sub'}, dimensions={0} | all-to-all | bytes 131072 | tf_op jit(solution)/shard_map/all_to_all | solution.py:427
  38.3 0.5 start.1
  38.8 2.7 %copy.16 = f32[128,1,2816]{2,1,0:T(1,128)} copy(f32[128,1,2816]{2,0,1:T(8,128)S(1)} %bitcast.38) | data formatting | bytes 2883584 | tf_op jit(solution)/shard_map/all_to_all | solution.py:443
  41.5 5.4 %all-to-all-start.1 = ((f32[128,1,2816]{2,1,0:T(1,128)}), f32[128,1,2816]{2,1,0:T(1,128)}, u32[]{:S(2)}, u32[]{:S(2)}) async-start(f32[128,1,2816]{2,1,0:T(1,128)} %copy.16), calls=%async_computation.1 | async-start | bytes 2883584 | tf_op jit(solution)/shard_map/all_to_all | solution.py:443
  46.9 0.1 pad.10.clone
  47.0 0.1 fusion.info
  47.0 25.5 %all-to-all-done.1 = f32[128,1,2816]{2,1,0:T(1,128)} async-done(((f32[128,1,2816]{2,1,0:T(1,128)}), f32[128,1,2816]{2,1,0:T(1,128)}, u32[]{:S(2)}, u32[]{:S(2)}) %all-to-all-start.1) | async-done | bytes 1441824 | tf_op jit(solution)/shard_map/all_to_all | solution.py:443
  72.5 1.5 copy.28
  74.0 0.0 copy-start.10
  74.0 2.5 %top.1 = f32[16,128,128]{2,1,0:T(8,128)S(1)} custom-call(s32[5,32]{1,0:T(8,128)S(1)} %fusion.info, f32[128,2816]{1,0:T(8,128)S(1)} %bitcast.34), custom_call_target="tpu_custom_call" | custom-call | tf_op jit(solution)/shard_map/top/pallas_call | solution.py:67
  76.5 1.0 copy-done.2
  77.4 3.6 %all-gather.3.cloned.1.call-done = f32[24,64,1024]{2,1,0:T(8,128)} async-done(((f32[3,64,1024]{2,1,0:T(8,128)}), f32[24,64,1024]{2,1,0:T(8,128)}) %all-gather.3.cloned.1.call-update) | async-done | bytes 6291472 | tf_op jit(solution)/shard_map/all_gather | solution.py:393
  81.1 18.8 %first.1 = (f32[1,1024]{1,0:T(1,128)S(1)}, f32[128,1408]{1,0:T(8,128)S(1)}, bf16[48,128,512]{2,1,0:T(8,128)(2,1)}, f32[8,128,128]{2,1,0:T(8,128)S(1)}) custom-call(s32[5,32]{1,0:T(8,128)S(1)} %fusion.info, f32[2]{0:T(128)S(1)} %copy-done.10, f32[8,3,64,1024]{3,2,1,0:T(8,128)} %bitcast.49, bf16[1024,256]{1,0:T(8,128)(2,1)S(1)} %get-tuple-element.19.lhs, ...), custom_call_target="tpu_custom_call" | custom-call | tf_op jit(solution)/shard_map/first/pallas_call | solution.py:67
  99.9 0.7 copy.17
  100.7 23.0 %all_to_all.56 = f32[128,1,1408]{2,1,0:T(1,128)S(1)} all-to-all(f32[128,1,1408]{2,1,0:T(1,128)S(1)} %copy.17), channel_id=1, replica_groups=mesh['leaf'=16,'sub'=8] {'leaf','sub'}, dimensions={0} | all-to-all | bytes 1441792 | tf_op jit(solution)/shard_map/all_to_all | solution.py:482
  123.8 13.2 %second.1 = f32[8,1024]{1,0:T(8,128)S(1)} custom-call(s32[5,32]{1,0:T(8,128)S(1)} %fusion.info, f32[2]{0:T(128)S(1)} %copy-done.10, bf16[1024,256]{1,0:T(8,128)(2,1)S(1)} %get-tuple-element.19.lhs, f32[1,1024]{1,0:T(1,128)S(1)} %get-tuple-element.20.u_row, f32[256,128]{1,0:T(8,128)S(1)} %get-tuple-element.21.uz_col, f32[2,128,512]{2,1,0:T(8,128)S(1)} %copy-done.4, ...), custom_call_target="tpu_custom_call" | custom-call | tf_op jit(solution)/shard_map/second/pallas_call | solution.py:67
  137.1 8.2 %all_to_all.57 = f32[8,1,1024]{2,1,0:T(1,128)S(1)} all-to-all(f32[8,1,1024]{2,1,0:T(1,128)S(1)} %copy.18), channel_id=1, replica_groups=mesh['leaf'=16,'sub'=8] {'sub'}, dimensions={0} | all-to-all | bytes 65536 | tf_op jit(solution)/shard_map/all_to_all | solution.py:504
  145.3 0.1 project.1
  145.4 13.5 %all_to_all.58 = f32[128,1,128]{2,1,0:T(1,128)S(1)} all-to-all(f32[128,1,128]{2,1,0:T(1,128)S(1)} %bitcast.45), channel_id=1, replica_groups=mesh['leaf'=16,'sub'=8] {'leaf','sub'}, dimensions={0} | all-to-all | bytes 131072 | tf_op jit(solution)/shard_map/all_to_all | solution.py:512
  158.9 0.7 finish.1
  159.6 0.5 slice_bitcast_fusion
  (33 shorter events, 0.2 us)
Async XLA Ops:
  7.2 19.1 %copy-start.11 = (f32[1024,64]{0,1:T(8,128)S(1)}, f32[1024,64]{0,1:T(8,128)}, u32[]{:S(2)}) copy-start(f32[1024,64]{0,1:T(8,128)} %param.11) | copy-start | bytes 786436
  7.2 73.9 %all-gather.3.cloned.1.call-start = ((), (), s32[]{:S(2)}) async-start(), calls=%async_computation.5 | async-start | bytes 7077888 | tf_op jit(solution)/shard_map/all_gather | solution.py:393
  8.2 11.8 %collective-permute-start.1 = (f32[64,1024]{1,0:T(8,128)S(1)}, f32[64,1024]{1,0:T(8,128)S(1)}, u32[]{:S(2)}, u32[]{:S(2)}) collective-permute-start(f32[64,1024]{1,0:T(8,128)S(1)} %get-tuple-element.37.qt), channel_id=1, source_target_pairs={{8,0},{16,8},{24,16},{32,24},{40,32},{48,40},{56,48},{64,56},{72,6... | collective-permute-start | bytes 786440 | tf_op jit(solution)/shard_map/ppermute | solution.py:392
  15.1 10.2 %collective-permute-start = (f32[64,1024]{1,0:T(8,128)S(1)}, f32[64,1024]{1,0:T(8,128)S(1)}, u32[]{:S(2)}, u32[]{:S(2)}) collective-permute-start(f32[64,1024]{1,0:T(8,128)S(1)} %get-tuple-element.37.qt), channel_id=1, source_target_pairs={{0,8},{8,16},{16,24},{24,32},{32,40},{40,48},{48,56},{56,64},{64,7... | collective-permute-start | bytes 786440 | tf_op jit(solution)/shard_map/ppermute | solution.py:391
  25.3 1.2 copy-start.14
  25.3 1.2 copy-start.6
  25.3 1.2 copy-start.8
  25.3 1.2 copy-start.9
  26.2 12.0 %copy-start.4 = (f32[2,128,512]{2,1,0:T(8,128)S(1)}, f32[2,128,512]{2,1,0:T(8,128)}, u32[]{:S(2)}) copy-start(f32[2,128,512]{2,1,0:T(8,128)} %lm.5) | copy-start | bytes 1572868
  26.2 12.0 %copy-start.5 = (f32[2,128,512]{2,1,0:T(8,128)S(1)}, f32[2,128,512]{2,1,0:T(8,128)}, u32[]{:S(2)}) copy-start(f32[2,128,512]{2,1,0:T(8,128)} %rm.5) | copy-start | bytes 1572868
  26.2 12.0 %copy-start.7 = (s32[1024]{0:T(1024)S(1)}, s32[1024]{0:T(1024)}, u32[]{:S(2)}) copy-start(s32[1024]{0:T(1024)} %param.17) | copy-start | bytes 12292
  41.5 5.5 %copy-start.12 = (s32[2,4]{1,0:T(2,128)S(1)}, s32[2,4]{1,0:T(2,128)}, u32[]{:S(2)}) copy-start(s32[2,4]{1,0:T(2,128)} %param.21) | copy-start | bytes 100
  41.5 5.5 %copy-start.13 = (s32[2,32]{1,0:T(2,128)S(1)}, s32[2,32]{1,0:T(2,128)}, u32[]{:S(2)}) copy-start(s32[2,32]{1,0:T(2,128)} %param.20) | copy-start | bytes 772
  41.5 31.0 %all-to-all-start.1 = ((f32[128,1,2816]{2,1,0:T(1,128)}), f32[128,1,2816]{2,1,0:T(1,128)}, u32[]{:S(2)}, u32[]{:S(2)}) async-start(f32[128,1,2816]{2,1,0:T(1,128)} %copy.16), calls=%async_computation.1 | async-start | bytes 2883584 | tf_op jit(solution)/shard_map/all_to_all | solution.py:443
  74.0 7.1 %copy-start = (f32[128,1,2816]{2,0,1:T(8,128)}, f32[128,1,2816]{2,0,1:T(8,128)S(1)}, u32[]{:S(2)}) copy-start(f32[128,1,2816]{2,0,1:T(8,128)S(1)} %copy.28) | copy-start | bytes 4325380
  74.0 7.1 %copy-start.10 = (f32[2]{0:T(128)S(1)}, f32[2]{0:T(128)}, u32[]{:S(2)}) copy-start(f32[2]{0:T(128)} %ritz.3) | copy-start | bytes 28
  76.5 1.0 copy-start.2
  100.6 23.1 %copy-start.3 = (f32[16,128,128]{2,1,0:T(8,128)S(1)}, f32[16,128,128]{2,1,0:T(8,128)}, u32[]{:S(2)}) copy-start(f32[16,128,128]{2,1,0:T(8,128)} %copy-done.2) | copy-start | bytes 3145732
  123.8 35.1 %copy-start.1 = (f32[128,1,2816]{2,0,1:T(8,128)S(1)}, f32[128,1,2816]{2,0,1:T(8,128)}, u32[]{:S(2)}) copy-start(f32[128,1,2816]{2,0,1:T(8,128)} %copy-done) | copy-start | bytes 4325380
Sparse Core Ops, SparseCore 0:
  26.4 54.6 all-gather.2

commit v3 on v2

--- a/solution.py
+++ b/solution.py
@@ -17,7 +17,7 @@
 BOTH = ("leaf", "sub")
 STEP = 256
 UNROLL = 8
-VMEM_LIMIT = 50 * 1024 * 1024
+MIB = 1024 * 1024
 NT = (((1,), (1,)), ((), ()))
 TN = (((0,), (0,)), ((), ()))
 
@@ -61,16 +61,18 @@
     return row, order & 127
 
 
-def call(body, outs, *args, smem=(), far=(), scratch=(), cost=None, name=None):
+def call(body, outs, *args, smem=(), far=(), hbm_outs=(), scratch=(), cost=None, name=None, room=6):
     places = [pltpu.SMEM if i in smem else pl.ANY if i in far else pltpu.VMEM for i in range(len(args))]
     specs = [pl.BlockSpec(memory_space=place) for place in places]
     return pl.pallas_call(
         body,
         out_shape=outs,
         in_specs=specs,
-        out_specs=[pl.BlockSpec(memory_space=pltpu.VMEM)] * len(outs),
+        out_specs=[
+            pl.BlockSpec(memory_space=pl.ANY if i in hbm_outs else pltpu.VMEM) for i in range(len(outs))
+        ],
         scratch_shapes=list(scratch),
-        compiler_params=pltpu.CompilerParams(vmem_limit_bytes=VMEM_LIMIT),
+        compiler_params=pltpu.CompilerParams(vmem_limit_bytes=room * MIB),
         cost_estimate=cost,
         name=name,
     )(*args)
@@ -124,7 +126,7 @@
     return [v * u_row[...]] + skel + [row_sums(root)]
 
 
-def start_kernel(got, order, u_row, uz_row, lm, rm, skel, gram, v_row, sent):
+def start_kernel(got, order, u_row, uz_row, lm, rm, skel, v_row, sent):
     subs = got.shape[0]
     count = order.shape[1]
     tiles = count // LANES
@@ -140,15 +142,15 @@
         sums.append(jnp.sum(got[:, at : at + LANES], axis=0, keepdims=True))
     skels = [skel[a : a + 1, :].astype(F32) for a in range(skel.shape[0])]
     block = jnp.concatenate(
-        packed_vector(v, u_row, uz_row, lm, rm) + skels + sums + [gram[...]], axis=1
-    )
-    sent[...] = jnp.broadcast_to(block, sent.shape)
+        packed_vector(v, u_row, uz_row, lm, rm) + skels + sums, axis=1
+    )
+    sent[...] = block
 
 
 def top_kernel(feats, info, tab, blocks):
     leaf_count, skel_count, _ = blocks.shape
     subs = tab.shape[0] // leaf_count
-    at = tab.shape[1] - LANES - feats // subs * skel_count
+    at = tab.shape[1] - feats // subs * skel_count
     me = info[info.shape[0] - 1, 0]
 
     def root_points(u):
@@ -270,7 +272,7 @@
 
 def first_kernel(
     counts, info, ritz, window, lhs, z_lhs, u_row, uz_row, uz_col, lm, rm, top, v_row, vec,
-    first_row, sent, split, far_blocks, landed, values, acc, sems,
+    first_row, sent, split_out, far_blocks, landed, split, values, acc, sems, out_sem,
 ):
     near_count, far_count = counts
     per_device, skel_count, leaf_size = lm.shape
@@ -290,6 +292,8 @@
                 slot = side * per_side + d * per_device + j
                 split[slot, :feats, :] = h
                 split[slot, feats:, :] = l
+    written = pltpu.make_async_copy(split, split_out, out_sem)
+    written.start()
     near_sums(info, split, values, lhs, acc, near_count)
     index_at = skel_at + skel_count
     for a in range(per_device):
@@ -304,20 +308,24 @@
     y = gathered(acc, u_row, uz_col, lm, rm, v_row, skel_out, root_out)
     first = v_row[...] - y / ritz[0]
     first_row[...] = first
+    written.wait()
     block = jnp.concatenate(packed_vector(first, u_row, uz_row, lm, rm), axis=1)
-    sent[...] = jnp.broadcast_to(block, sent.shape)
+    sent[...] = block
 
 
 def second_kernel(
-    counts, info, ritz, lhs, u_row, uz_col, lm, rm, top, split, far_blocks, v_row, vec, tree_row, order,
-    sent, values, acc,
+    counts, info, ritz, lhs, u_row, uz_col, lm, rm, top, split_in, far_blocks, v_row, vec, tree_row, order,
+    sent, values, acc, split, sems,
 ):
     near_count, far_count = counts
     per_device, skel_count, leaf_size = lm.shape
     subs, count = sent.shape
+    read = pltpu.make_async_copy(split_in, split, sems)
+    read.start()
     spread_values(info, vec, values, subs, leaf_size)
     root_out = top_sums(top, vec, subs, count + per_device * skel_count)
     skel_out = far_sums(info, far_blocks, vec, far_count, subs, subs * per_device, count)
+    read.wait()
     near_sums(info, split, values, lhs, acc, near_count)
     y = gathered(acc, u_row, uz_col, lm, rm, v_row, skel_out, root_out)
     grown = tree_row[...] - (v_row[...] - y / ritz[1])
@@ -330,7 +338,7 @@
         sent[:, k * LANES : (k + 1) * LANES] = placed[k * subs : (k + 1) * subs]
 
 
-def project_kernel(got, basis, user_row, sent):
+def project_kernel(got, basis, gram, user_row, sent):
     user = jnp.sum(got[...], axis=0, keepdims=True)
     user_row[...] = user
     b = basis[...]
@@ -341,15 +349,14 @@
     sub = lax.broadcasted_iota(jnp.int32, (vecs, LANES), 0)
     row = jnp.sum(jnp.where(lane == sub, proj, 0.0), axis=0, keepdims=True)
     row = row + jnp.where(lane[:1] == vecs, norm, 0.0)
-    sent[...] = jnp.broadcast_to(row, sent.shape)
-
-
-def finish_kernel(got, tab, basis, user_row, orth, hess):
+    sent[...] = jnp.concatenate([row, gram[...]], axis=1)
+
+
+def finish_kernel(got, basis, user_row, orth, hess):
     b = basis[...]
     vecs = b.shape[0]
     total = jnp.sum(got[...], axis=0, keepdims=True)
-    width = tab.shape[1]
-    gram = jnp.sum(tab[:, width - LANES :], axis=0, keepdims=True)
+    total, gram = total[:, :LANES], total[:, LANES:]
     lane = lax.broadcasted_iota(jnp.int32, (vecs, LANES), 1)
     sub = lax.broadcasted_iota(jnp.int32, (vecs, LANES), 0)
     proj = jnp.sum(jnp.where(lane == sub, total, 0.0), axis=1, keepdims=True)
@@ -362,6 +369,10 @@
     length = jnp.sqrt(jnp.maximum(norm - 2.0 * cross + quad, 0.0) + EPSILON)
     orth[...] = user_row[...] - jnp.sum(proj * b, axis=0, keepdims=True)
     hess[...] = jnp.where(one < vecs, total, jnp.broadcast_to(length, (1, LANES)))
+
+
+def to_all(row, everyone):
+    return lax.all_to_all(jnp.broadcast_to(row, (everyone, row.shape[1])), BOTH, 0, 0, tiled=True)
 
 
 def shards(
@@ -426,10 +437,10 @@
     )
     got = lax.all_to_all(sent, "sub", 0, 0, tiled=True)
     vec_width = count + per_device * skel_count + skel_count
-    tab_width = vec_width + per_device * skel_count + (feats // subs) * skel_count + LANES
+    tab_width = vec_width + per_device * skel_count + (feats // subs) * skel_count
     tree_row, sent = call(
         start_kernel,
-        [sds((1, count), F32), sds((everyone, tab_width), F32)],
+        [sds((1, count), F32), sds((1, tab_width), F32)],
         got,
         order,
         u_row,
@@ -437,10 +448,9 @@
         leaf_maps,
         root_maps,
         skeleton,
-        gram,
         name="start",
     )
-    tab = lax.all_to_all(sent, BOTH, 0, 0, tiled=True)
+    tab = to_all(sent, everyone)
     (top,) = call(
         functools.partial(top_kernel, feats),
         [sds((leaves, skel_count, skel_count), F32)],
@@ -453,11 +463,12 @@
     counts = (near_count, far_count)
     spread = pltpu.VMEM((slots, 8, leaf_size), F32)
     sums = pltpu.VMEM((count, LANES), F32)
+    halved = pltpu.VMEM((slots, 2 * feats, leaf_size), BF16)
     first_row, sent, split, far_blocks = call(
         functools.partial(first_kernel, counts),
         [
             sds((1, count), F32),
-            sds((everyone, vec_width), F32),
+            sds((1, vec_width), F32),
             sds((slots, 2 * feats, leaf_size), BF16),
             sds((per_device * far_count, skel_count, skel_count), F32),
         ],
@@ -476,10 +487,19 @@
         tab,
         smem=(0, 1),
         far=(2,),
-        scratch=[pltpu.VMEM(window.shape, F32), spread, sums, pltpu.SemaphoreType.DMA((subs,))],
+        hbm_outs=(2,),
+        scratch=[
+            pltpu.VMEM(window.shape, F32),
+            halved,
+            spread,
+            sums,
+            pltpu.SemaphoreType.DMA((subs,)),
+            pltpu.SemaphoreType.DMA,
+        ],
+        room=58,
         name="first",
     )
-    vec = lax.all_to_all(sent, BOTH, 0, 0, tiled=True)
+    vec = to_all(sent, everyone)
     (sent,) = call(
         functools.partial(second_kernel, counts),
         [sds((subs, count), F32)],
@@ -498,23 +518,25 @@
         tree_row,
         order,
         smem=(0, 1),
-        scratch=[spread, sums],
+        far=(8,),
+        scratch=[spread, sums, halved, pltpu.SemaphoreType.DMA],
+        room=58,
         name="second",
     )
     got = lax.all_to_all(sent, "sub", 0, 0, tiled=True)
     user_row, sent = call(
         project_kernel,
-        [sds((1, count), F32), sds((everyone, LANES), F32)],
+        [sds((1, count), F32), sds((1, 2 * LANES), F32)],
         got,
         krylov_basis,
+        gram,
         name="project",
     )
-    got = lax.all_to_all(sent, BOTH, 0, 0, tiled=True)
+    got = to_all(sent, everyone)
     orth, hess = call(
         finish_kernel,
         [sds((1, count), F32), sds((1, LANES), F32)],
         got,
-        tab,
         krylov_basis,
         user_row,
         name="finish",

time: 167 us -> 171 us (1.024)
  local copies, waits for them, and re-layouts: 6.86 us -> 10.1 us
  waiting for transfers between devices: 39.3 us -> 36.4 us
    unnamed x35 -> x44, local copies, waits for them, and re-layouts: 2.74 us -> 6.36 us
    all_to_all x2 -> x0, local copies, waits for them, and re-layouts: 3.43 us -> none  [the longest x1 2.69 us: shards(): tab = lax.all_to_all(sent, BOTH, 0, 0, tiled=True)]
    broadcast_in_dim x0 -> x3, local copies, waits for them, and re-layouts: none -> 2.33 us  [to_all(): jnp.broadcast_to(row, (everyone, row.shape[1]))]
    all_gather x1, waiting for transfers between devices: 3.63 us -> 1.62 us  [shards(): window = lax.all_gather(jnp.stack([low, qt, high]), 'sub', axis=0)]
  transfers between devices with their start and end apart: 4 -> 4, of which waited for: 4 -> 4; matrix products, arithmetic and copies ran while one was open for 3% -> 2% of each run, Pallas kernels for 2% -> 2%
where the time goes in v3:
time: 171 us; the launch traced here: 170 us
  blocking collectives  56.4 us (33%)
  Pallas kernels  37.9 us (22%)
  waiting for transfers between devices  36.4 us (21%)
  between operations  14.3 us (8%)
  starting transfers between devices  12.4 us (7%)
  local copies, waits for them, and re-layouts  10.1 us (6%)
  other arithmetic  2.75 us (2%)
    pallas_call x7, Pallas kernels, call(): pl.pallas_call(body, out_shape=outs, in_specs=specs, out_specs=[pl.BlockS...  37.9 us
    all_to_all x2, blocking collectives, to_all(): lax.all_to_all(jnp.broadcast_to(row, (everyone, row.shape[1])), BOTH, 0,...  36.6 us
    all_to_all x1, waiting for transfers between devices, to_all(): lax.all_to_all(jnp.broadcast_to(row, (everyone, row.shape[1])), BOTH, 0,...  24.6 us
    all_to_all x2, blocking collectives, shards(): got = lax.all_to_all(sent, 'sub', 0, 0, tiled=True)  19.8 us
    ppermute x1, starting transfers between devices, shards(): high = lax.ppermute(qt, 'leaf', back)  6.85 us
    unnamed x44, local copies, waits for them, and re-layouts  6.36 us
    all_to_all x1, starting transfers between devices, to_all(): lax.all_to_all(jnp.broadcast_to(row, (everyone, row.shape[1])), BOTH, 0,...  5.53 us
    ppermute x1, waiting for transfers between devices, shards(): low = lax.ppermute(qt, 'leaf', ring)  5.2 us
  transfers between devices with their start and end apart: 4, of which 4 were waited for; matrix products, arithmetic and copies ran while one was open for 2% of the time, Pallas kernels for 2%

profile of v3, /device:TPU:1, one launch (start us, length us, event | category | flops | bytes accessed | tf_op | source)
XLA Modules:
  0.0 170.2 jit_solution(986113401970788826)
XLA Ops:
  7.2 1.0 multiply_bitcast_fusion
  8.2 6.8 %collective-permute-start.1 = (f32[64,1024]{1,0:T(8,128)S(1)}, f32[64,1024]{1,0:T(8,128)S(1)}, u32[]{:S(2)}, u32[]{:S(2)}) collective-permute-start(f32[64,1024]{1,0:T(8,128)S(1)} %get-tuple-element.37.qt), channel_id=1, source_target_pairs={{8,0},{16,8},{24,16},{32,24},{40,32},{48,40},{56,48},{64,56},{72,6... | collective-permute-start | bytes 786440 | tf_op jit(solution)/shard_map/ppermute | solution.py:403
  15.1 5.0 %collective-permute-done.1 = f32[64,1024]{1,0:T(8,128)S(1)} collective-permute-done((f32[64,1024]{1,0:T(8,128)S(1)}, f32[64,1024]{1,0:T(8,128)S(1)}, u32[]{:S(2)}, u32[]{:S(2)}) %collective-permute-start.1) | collective-permute-done | bytes 262176 | tf_op jit(solution)/shard_map/ppermute | solution.py:403
  20.0 5.2 %collective-permute-done = f32[64,1024]{1,0:T(8,128)S(1)} collective-permute-done((f32[64,1024]{1,0:T(8,128)S(1)}, f32[64,1024]{1,0:T(8,128)S(1)}, u32[]{:S(2)}, u32[]{:S(2)}) %collective-permute-start) | collective-permute-done | bytes 262176 | tf_op jit(solution)/shard_map/ppermute | solution.py:402
  25.2 0.9 pad_maximum_fusion
  26.2 0.2 copy.14.pts
  26.5 0.6 prepare.1
  27.1 0.8 copy-done.4
  27.9 0.6 copy-done.5
  28.6 0.7 copy-done.7
  29.3 11.5 %all_to_all.46 = f32[8,1,2048]{2,1,0:T(1,128)S(1)} all-to-all(f32[8,1,2048]{2,1,0:T(1,128)S(1)} %copy.15), channel_id=1, replica_groups=mesh['leaf'=16,'sub'=8] {'sub'}, dimensions={0} | all-to-all | bytes 131072 | tf_op jit(solution)/shard_map/all_to_all | solution.py:438
  40.9 0.5 start.1
  41.5 0.6 copy-done.11
  42.1 1.9 %broadcast_in_dim.9 = f32[128,1,2688]{2,1,0:T(1,128)} broadcast(f32[2688]{0:T(1024)S(1)} %reduce), dimensions={2} | broadcast | bytes 1387008 | tf_op jit(solution)/shard_map/broadcast_in_dim | solution.py:375
  44.0 5.5 %all-to-all-start.1 = ((f32[128,1,2688]{2,1,0:T(1,128)}), f32[128,1,2688]{2,1,0:T(1,128)}, u32[]{:S(2)}, u32[]{:S(2)}) async-start(f32[128,1,2688]{2,1,0:T(1,128)} %broadcast_in_dim.9), calls=%async_computation.1 | async-start | bytes 2752512 | tf_op jit(solution)/shard_map/all_to_all | solution.py:375
  49.7 24.6 %all-to-all-done.1 = f32[128,1,2688]{2,1,0:T(1,128)} async-done(((f32[128,1,2688]{2,1,0:T(1,128)}), f32[128,1,2688]{2,1,0:T(1,128)}, u32[]{:S(2)}, u32[]{:S(2)}) %all-to-all-start.1) | async-done | bytes 1376288 | tf_op jit(solution)/shard_map/all_to_all | solution.py:375
  74.3 1.4 copy.27
  75.7 2.5 %top.1 = f32[16,128,128]{2,1,0:T(8,128)S(1)} custom-call(s32[5,32]{1,0:T(8,128)S(1)} %fusion.info, f32[128,2688]{1,0:T(8,128)S(1)} %bitcast.32), custom_call_target="tpu_custom_call" | custom-call | tf_op jit(solution)/shard_map/top/pallas_call | solution.py:67
  78.2 0.9 copy-done.1
  79.1 1.6 all-gather.3.cloned.1.call-done
  80.8 17.7 %first.1 = (f32[1,1024]{1,0:T(1,128)}, f32[1,1408]{1,0:T(1,128)}, bf16[48,128,512]{2,1,0:T(8,128)(2,1)}, f32[8,128,128]{2,1,0:T(8,128)}) custom-call(s32[5,32]{1,0:T(8,128)} %copy-done.8, f32[2]{0:T(128)} %ritz.3, f32[8,3,64,1024]{3,2,1,0:T(8,128)} %bitcast.42, bf16[1024,256]{1,0:T(8,128)(2,1)} %copy-done.4, bf16[256,256]{1,0:T(8,128)(2,1)} %copy-done.7, ...), custom_call_target="tpu_custom_call" | custom-call | tf_op jit(solution)/shard_map/first/pallas_call | solution.py:67
  98.5 0.7 reduce.1
  99.2 0.4 broadcast_in_dim.20
  99.6 22.6 %all_to_all.47 = f32[128,1,1408]{2,1,0:T(1,128)S(1)} all-to-all(f32[128,1,1408]{2,1,0:T(1,128)S(1)} %broadcast_in_dim.20), channel_id=1, replica_groups=mesh['leaf'=16,'sub'=8] {'leaf','sub'}, dimensions={0} | all-to-all | bytes 1441792 | tf_op jit(solution)/shard_map/all_to_all | solution.py:375
  122.1 1.0 copy.28
  123.1 15.8 %second.1 = f32[8,1024]{1,0:T(8,128)} custom-call(s32[5,32]{1,0:T(8,128)} %copy-done.8, f32[2]{0:T(128)} %ritz.3, bf16[1024,256]{1,0:T(8,128)(2,1)} %copy-done.4, f32[1,1024]{1,0:T(1,128)} %copy-done.9, f32[256,128]{1,0:T(8,128)} %copy-done.5, f32[2,128,512]{2,1,0:T(8,128)} %lm.5, f32[2,128,512]{2,1,0:T(8,128)} %rm.5, f32[16,128,128]{2,1,0:T(8,128)} %copy-done.1, ...), custom_call_target="tpu_custom_call" | custom-call | tf_op jit(solution)/shard_map/second/pallas_call | solution.py:67
  138.9 0.8 copy.16
  139.7 8.3 %all_to_all.48 = f32[8,1,1024]{2,1,0:T(1,128)S(1)} all-to-all(f32[8,1,1024]{2,1,0:T(1,128)S(1)} %copy.16), channel_id=1, replica_groups=mesh['leaf'=16,'sub'=8] {'sub'}, dimensions={0} | all-to-all | bytes 65536 | tf_op jit(solution)/shard_map/all_to_all | solution.py:526
  148.0 0.1 project.1
  148.1 14.0 %all_to_all.49 = f32[128,1,256]{2,1,0:T(1,128)S(1)} all-to-all(f32[128,1,256]{2,1,0:T(1,128)S(1)} %broadcast_in_dim.21), channel_id=1, replica_groups=mesh['leaf'=16,'sub'=8] {'leaf','sub'}, dimensions={0} | all-to-all | bytes 262144 | tf_op jit(solution)/shard_map/all_to_all | solution.py:375
  162.2 0.7 finish.1
  162.9 0.5 slice_bitcast_fusion
  (45 shorter events, 0.5 us)
Async XLA Ops:
  7.2 73.6 %all-gather.3.cloned.1.call-start = ((), (), s32[]{:S(2)}) async-start(), calls=%async_computation.5 | async-start | bytes 7077888 | tf_op jit(solution)/shard_map/all_gather | solution.py:404
  8.2 18.0 %copy-start.15 = (f32[1024,64]{0,1:T(8,128)S(1)}, f32[1024,64]{0,1:T(8,128)}, u32[]{:S(2)}) copy-start(f32[1024,64]{0,1:T(8,128)} %param.11) | copy-start | bytes 786436
  8.2 11.8 %collective-permute-start.1 = (f32[64,1024]{1,0:T(8,128)S(1)}, f32[64,1024]{1,0:T(8,128)S(1)}, u32[]{:S(2)}, u32[]{:S(2)}) collective-permute-start(f32[64,1024]{1,0:T(8,128)S(1)} %get-tuple-element.37.qt), channel_id=1, source_target_pairs={{8,0},{16,8},{24,16},{32,24},{40,32},{48,40},{56,48},{64,56},{72,6... | collective-permute-start | bytes 786440 | tf_op jit(solution)/shard_map/ppermute | solution.py:403
  15.1 10.2 %collective-permute-start = (f32[64,1024]{1,0:T(8,128)S(1)}, f32[64,1024]{1,0:T(8,128)S(1)}, u32[]{:S(2)}, u32[]{:S(2)}) collective-permute-start(f32[64,1024]{1,0:T(8,128)S(1)} %get-tuple-element.37.qt), channel_id=1, source_target_pairs={{0,8},{8,16},{16,24},{24,32},{32,40},{40,48},{48,56},{56,64},{64,7... | collective-permute-start | bytes 786440 | tf_op jit(solution)/shard_map/ppermute | solution.py:402
  25.2 1.2 copy-start.18
  25.2 1.2 copy-start.6
  25.2 1.2 copy-start.12
  25.2 1.2 copy-start.13
  26.2 14.7 %copy-start.2 = (f32[2,128,512]{2,1,0:T(8,128)S(1)}, f32[2,128,512]{2,1,0:T(8,128)}, u32[]{:S(2)}) copy-start(f32[2,128,512]{2,1,0:T(8,128)} %lm.5) | copy-start | bytes 1572868
  26.2 14.7 %copy-start.3 = (f32[2,128,512]{2,1,0:T(8,128)S(1)}, f32[2,128,512]{2,1,0:T(8,128)}, u32[]{:S(2)}) copy-start(f32[2,128,512]{2,1,0:T(8,128)} %rm.5) | copy-start | bytes 1572868
  26.2 14.7 %copy-start.10 = (s32[1024]{0:T(1024)S(1)}, s32[1024]{0:T(1024)}, u32[]{:S(2)}) copy-start(s32[1024]{0:T(1024)} %param.17) | copy-start | bytes 12292
  27.1 0.8 copy-start.4
  27.9 0.6 copy-start.5
  28.6 0.7 copy-start.7
  29.3 14.7 %copy-start.9 = (f32[1,1024]{1,0:T(1,128)}, f32[1,1024]{1,0:T(1,128)S(1)}, u32[]{:S(2)}) copy-start(f32[1,1024]{1,0:T(1,128)S(1)} %get-tuple-element.20.u_row) | copy-start | bytes 12292
  29.3 14.7 %copy-start.14 = (f32[2,128]{1,0:T(2,128)}, f32[2,128]{1,0:T(2,128)S(1)}, u32[]{:S(2)}) copy-start(f32[2,128]{1,0:T(2,128)S(1)} %get-tuple-element.23.uz_row) | copy-start | bytes 3076
  41.5 0.6 copy-start.11
  44.0 5.6 %copy-start.16 = (s32[2,4]{1,0:T(2,128)S(1)}, s32[2,4]{1,0:T(2,128)}, u32[]{:S(2)}) copy-start(s32[2,4]{1,0:T(2,128)} %param.21) | copy-start | bytes 100
  44.0 5.6 %copy-start.17 = (s32[2,32]{1,0:T(2,128)S(1)}, s32[2,32]{1,0:T(2,128)}, u32[]{:S(2)}) copy-start(s32[2,32]{1,0:T(2,128)} %param.20) | copy-start | bytes 772
  44.0 30.3 %all-to-all-start.1 = ((f32[128,1,2688]{2,1,0:T(1,128)}), f32[128,1,2688]{2,1,0:T(1,128)}, u32[]{:S(2)}, u32[]{:S(2)}) async-start(f32[128,1,2688]{2,1,0:T(1,128)} %broadcast_in_dim.9), calls=%async_computation.1 | async-start | bytes 2752512 | tf_op jit(solution)/shard_map/all_to_all | solution.py:375
  49.7 26.0 %copy-start.8 = (s32[5,32]{1,0:T(8,128)}, s32[5,32]{1,0:T(8,128)S(1)}, u32[]{:S(2)}) copy-start(s32[5,32]{1,0:T(8,128)S(1)} %fusion.info) | copy-start | bytes 1924
  75.7 5.1 %copy-start = (f32[128,1,2688]{2,0,1:T(8,128)}, f32[128,1,2688]{2,0,1:T(8,128)S(1)}, u32[]{:S(2)}) copy-start(f32[128,1,2688]{2,0,1:T(8,128)S(1)} %copy.27) | copy-start | bytes 4128772
  78.2 1.0 copy-start.1
Sparse Core Ops, SparseCore 0:
  26.3 54.3 all-gather.2

commit v4 on v3

--- a/solution.py
+++ b/solution.py
@@ -61,7 +61,7 @@
     return row, order & 127
 
 
-def call(body, outs, *args, smem=(), far=(), hbm_outs=(), scratch=(), cost=None, name=None, room=6):
+def call(body, outs, *args, smem=(), far=(), hbm_outs=(), scratch=(), cost=None, name=None, room=50):
     places = [pltpu.SMEM if i in smem else pl.ANY if i in far else pltpu.VMEM for i in range(len(args))]
     specs = [pl.BlockSpec(memory_space=place) for place in places]
     return pl.pallas_call(
@@ -78,13 +78,9 @@
     )(*args)
 
 
-def prepare_kernel(
-    scale, leaf_size, pts, qt, skel, rskel, cur, basis, lhs, u_row, z_lhs, uz_row, uz_col, sent, gram
-):
+def prepare_kernel(leaf_size, qt, skel, rskel, cur, u_row, z_lhs, uz_row, uz_col, sent):
     per_device, skel_count = skel.shape
     feats, count = qt.shape
-    ph, pl_ = halves(pts[...] * scale)
-    lhs[...] = jnp.concatenate([ph, pl_, ph, pl_], axis=1)
     qh, ql = halves(qt[...])
     u_row[...] = half_norm(qh, ql)
     both = jnp.concatenate([qh, ql], axis=0)
@@ -106,12 +102,18 @@
     sent[:, :count] = jnp.broadcast_to(cur[...], (subs, count))
     for f in range(feats // subs):
         sent[:, count + f * LANES : count + (f + 1) * LANES] = r[f * subs : (f + 1) * subs]
+
+
+def own_kernel(scale, pts, basis, lhs, gram):
+    ph, pl_ = halves(pts[...] * scale)
+    lhs[...] = jnp.concatenate([ph, pl_, ph, pl_], axis=1)
     g = dot(basis[...], basis[...], NT, HI)
     vecs = basis.shape[0]
     lane = lax.broadcasted_iota(jnp.int32, (vecs, LANES), 1)
     sub = lax.broadcasted_iota(jnp.int32, (vecs, LANES), 0)
     wide = dot(g, ((lane & (vecs - 1)) == sub).astype(F32), precision=HI)
-    gram[...] = jnp.sum(jnp.where(lane // vecs == sub, wide, 0.0), axis=0, keepdims=True)
+    first = LANES - vecs * vecs
+    gram[...] = jnp.sum(jnp.where((lane - first) // vecs == sub, wide, 0.0), axis=0, keepdims=True)
 
 
 def packed_vector(v, u_row, uz_row, lm, rm):
@@ -126,7 +128,7 @@
     return [v * u_row[...]] + skel + [row_sums(root)]
 
 
-def start_kernel(got, order, u_row, uz_row, lm, rm, skel, v_row, sent):
+def start_kernel(got, order, u_row, uz_row, lm, rm, skel, v_row, near_sent, far_sent):
     subs = got.shape[0]
     count = order.shape[1]
     tiles = count // LANES
@@ -141,10 +143,9 @@
         at = count + k * LANES
         sums.append(jnp.sum(got[:, at : at + LANES], axis=0, keepdims=True))
     skels = [skel[a : a + 1, :].astype(F32) for a in range(skel.shape[0])]
-    block = jnp.concatenate(
-        packed_vector(v, u_row, uz_row, lm, rm) + skels + sums, axis=1
-    )
-    sent[...] = block
+    *near, root = packed_vector(v, u_row, uz_row, lm, rm)
+    near_sent[...] = jnp.concatenate(near + skels, axis=1)
+    far_sent[...] = jnp.concatenate([root] + sums, axis=1)
 
 
 def top_kernel(feats, info, tab, blocks):
@@ -174,38 +175,38 @@
     lax.fori_loop(0, leaf_count, subtree, 0, unroll=2)
 
 
-def owners(info, leaf_count, sides):
+def side_blocks(info, vec, subs, sides, start, stop):
+    leaf_count = vec.shape[0] // subs
     me = info[info.shape[0] - 1, 0]
-    return [(me + side + leaf_count - 1) % leaf_count for side in range(sides)]
-
-
-def spread_values(info, vec, values, subs, leaf_size):
-    slots = values.shape[0]
-    leaf_count = vec.shape[0] // subs
-    per_side = slots // 3
-    for side, owner in enumerate(owners(info, leaf_count, 3)):
-        block = vec[pl.ds(pl.multiple_of(owner * subs, subs), subs), : per_side // subs * leaf_size]
-        for n in range(per_side):
-            dev, j = n // (per_side // subs), n % (per_side // subs)
-            row = block[dev : dev + 1, j * leaf_size : (j + 1) * leaf_size]
-            values[side * per_side + n] = jnp.broadcast_to(row, (8, leaf_size))
-
-
-def picked_row(ref, info, slot, per_side, subs, offset, size):
-    leaf_count = ref.shape[0] // subs
-    me = info[info.shape[0] - 1, 0]
-    per_device = per_side // subs
-    side, n = slot // per_side, slot % per_side
-    owner = (me + side + leaf_count - 1) % leaf_count
-    rows = pl.ds(pl.multiple_of(owner * subs, subs), subs)
-    block = ref[rows, offset : offset + per_device * size]
+    blocks = []
+    for side in range(sides):
+        owner = (me + side + leaf_count - 1) % leaf_count
+        blocks.append(vec[pl.ds(pl.multiple_of(owner * subs, subs), subs), start:stop])
+    return blocks
+
+
+def spread_values(blocks, values):
+    leaf_size = values.shape[2]
+    subs, count = blocks[0].shape
+    slot = 0
+    for block in blocks:
+        for dev in range(subs):
+            for at in range(0, count, leaf_size):
+                row = block[dev : dev + 1, at : at + leaf_size]
+                values[slot] = jnp.broadcast_to(row, (8, leaf_size))
+                slot += 1
+
+
+def picked_row(blocks, slot, size):
+    subs, width = blocks[0].shape
+    per_device = width // size
     sub = lax.broadcasted_iota(jnp.int32, (subs, size), 0)
-    out = jnp.zeros((1, size), F32)
-    for j in range(per_device):
-        mine = (sub == n // per_device) & (n % per_device == j)
-        part = block[:, j * size : (j + 1) * size]
-        out = out + jnp.sum(jnp.where(mine, part, 0.0), axis=0, keepdims=True)
-    return out
+    out = jnp.zeros((subs, size), F32)
+    for side, block in enumerate(blocks):
+        for j in range(per_device):
+            mine = (side * subs + sub) * per_device + j == slot
+            out = jnp.where(mine, block[:, j * size : (j + 1) * size], out)
+    return jnp.sum(out, axis=0, keepdims=True)
 
 
 def quad(pair):
@@ -235,15 +236,14 @@
     lax.fori_loop(0, near_count, visit, 0, unroll=UNROLL)
 
 
-def far_sums(info, far_blocks, vec, far_count, subs, per_side, offset):
+def far_sums(info, far_blocks, blocks, far_count):
     per_device = (info.shape[0] - 1) // 2
     skel_count = far_blocks.shape[1]
     outs = []
     for a in range(per_device):
         total = jnp.zeros((skel_count, LANES), F32)
         for n in range(far_count):
-            slot = info[per_device + a, n]
-            w = picked_row(vec, info, slot, per_side, subs, offset, skel_count)
+            w = picked_row(blocks, info[per_device + a, n], skel_count)
             total = total + far_blocks[a * far_count + n] * w
         outs.append(jnp.sum(total, axis=1, keepdims=True))
     return outs
@@ -271,7 +271,7 @@
 
 
 def first_kernel(
-    counts, info, ritz, window, lhs, z_lhs, u_row, uz_row, uz_col, lm, rm, top, v_row, vec,
+    counts, info, ritz, window, lhs, z_lhs, u_row, uz_row, uz_col, lm, rm, top, v_row, vec, tab,
     first_row, sent, split_out, far_blocks, landed, split, values, acc, sems, out_sem,
 ):
     near_count, far_count = counts
@@ -281,9 +281,14 @@
     copies = [pltpu.make_async_copy(window.at[d], landed.at[d], sems.at[d]) for d in range(subs)]
     for copy in copies:
         copy.start()
-    spread_values(info, vec, values, subs, leaf_size)
-    skel_at = count + per_device * skel_count
-    root_out = top_sums(top, vec, subs, skel_at)
+    width = vec.shape[1] // sides
+    skels = per_device * skel_count
+
+    def sides_of(start, size):
+        return [vec[:, side * width + start : side * width + start + size] for side in range(sides)]
+
+    spread_values(sides_of(0, count), values)
+    root_out = top_sums(top, tab, subs, 0)
     for d in range(subs):
         copies[d].wait()
         for side in range(sides):
@@ -295,16 +300,15 @@
     written = pltpu.make_async_copy(split, split_out, out_sem)
     written.start()
     near_sums(info, split, values, lhs, acc, near_count)
-    index_at = skel_at + skel_count
+    indices = sides_of(count + skels, skels)
     for a in range(per_device):
         for n in range(far_count):
             slot = info[per_device + a, n]
-            index = picked_row(vec, info, slot, per_side, subs, index_at, skel_count).astype(jnp.int32)
-            hot = pick(index, leaf_size).astype(F32).astype(BF16)
-            z = dot(split[slot], hot).astype(BF16)
+            hot = pick(picked_row(indices, slot, skel_count).astype(jnp.int32), leaf_size)
+            z = dot(split[slot], hot.astype(F32).astype(BF16)).astype(BF16)
             left = z_lhs[a * skel_count : (a + 1) * skel_count, :]
             far_blocks[a * far_count + n] = jnp.exp2(dot(left, quad(z)))
-    skel_out = far_sums(info, far_blocks, vec, far_count, subs, per_side, count)
+    skel_out = far_sums(info, far_blocks, sides_of(count, skels), far_count)
     y = gathered(acc, u_row, uz_col, lm, rm, v_row, skel_out, root_out)
     first = v_row[...] - y / ritz[0]
     first_row[...] = first
@@ -314,18 +318,18 @@
 
 
 def second_kernel(
-    counts, info, ritz, lhs, u_row, uz_col, lm, rm, top, split_in, far_blocks, v_row, vec, tree_row, order,
-    sent, values, acc, split, sems,
+    counts, info, ritz, lhs, u_row, uz_col, lm, rm, top, split, far_blocks, v_row, vec, tree_row, order,
+    sent, values, acc,
 ):
     near_count, far_count = counts
     per_device, skel_count, leaf_size = lm.shape
     subs, count = sent.shape
-    read = pltpu.make_async_copy(split_in, split, sems)
-    read.start()
-    spread_values(info, vec, values, subs, leaf_size)
-    root_out = top_sums(top, vec, subs, count + per_device * skel_count)
-    skel_out = far_sums(info, far_blocks, vec, far_count, subs, subs * per_device, count)
-    read.wait()
+    sides = values.shape[0] // (subs * per_device)
+    skels = per_device * skel_count
+    spread_values(side_blocks(info, vec, subs, sides, 0, count), values)
+    root_out = top_sums(top, vec, subs, count + skels)
+    far_weights = side_blocks(info, vec, subs, sides, count, count + skels)
+    skel_out = far_sums(info, far_blocks, far_weights, far_count)
     near_sums(info, split, values, lhs, acc, near_count)
     y = gathered(acc, u_row, uz_col, lm, rm, v_row, skel_out, root_out)
     grown = tree_row[...] - (v_row[...] - y / ritz[1])
@@ -349,23 +353,23 @@
     sub = lax.broadcasted_iota(jnp.int32, (vecs, LANES), 0)
     row = jnp.sum(jnp.where(lane == sub, proj, 0.0), axis=0, keepdims=True)
     row = row + jnp.where(lane[:1] == vecs, norm, 0.0)
-    sent[...] = jnp.concatenate([row, gram[...]], axis=1)
+    sent[...] = row + gram[...]
 
 
 def finish_kernel(got, basis, user_row, orth, hess):
     b = basis[...]
     vecs = b.shape[0]
     total = jnp.sum(got[...], axis=0, keepdims=True)
-    total, gram = total[:, :LANES], total[:, LANES:]
     lane = lax.broadcasted_iota(jnp.int32, (vecs, LANES), 1)
     sub = lax.broadcasted_iota(jnp.int32, (vecs, LANES), 0)
     proj = jnp.sum(jnp.where(lane == sub, total, 0.0), axis=1, keepdims=True)
-    left = jnp.sum(jnp.where(lane // vecs == sub, proj, 0.0), axis=0, keepdims=True)
+    first = LANES - vecs * vecs
+    left = jnp.sum(jnp.where((lane - first) // vecs == sub, proj, 0.0), axis=0, keepdims=True)
     right = jnp.sum(jnp.where((lane & (vecs - 1)) == sub, proj, 0.0), axis=0, keepdims=True)
     one = lane[:1]
     norm = jnp.sum(jnp.where(one == vecs, total, 0.0), axis=1, keepdims=True)
     cross = jnp.sum(jnp.where(one < vecs, total * total, 0.0), axis=1, keepdims=True)
-    quad = jnp.sum(left * right * gram, axis=1, keepdims=True)
+    quad = jnp.sum(left * right * total, axis=1, keepdims=True)
     length = jnp.sqrt(jnp.maximum(norm - 2.0 * cross + quad, 0.0) + EPSILON)
     orth[...] = user_row[...] - jnp.sum(proj * b, axis=0, keepdims=True)
     hess[...] = jnp.where(one < vecs, total, jnp.broadcast_to(length, (1, LANES)))
@@ -401,7 +405,6 @@
     back = [(j, i) for i, j in ring]
     low = lax.ppermute(qt, "leaf", ring)
     high = lax.ppermute(qt, "leaf", back)
-    window = lax.all_gather(jnp.stack([low, qt, high]), "sub", axis=0)
 
     sds = jax.ShapeDtypeStruct
     near_count, far_count = near_list.shape[1], far_list.shape[1]
@@ -416,31 +419,41 @@
     order = point_order.reshape(1, count)
     rskel = root_skeleton - lax.axis_index("sub") * count
 
-    lhs, u_row, z_lhs, uz_row, uz_col, sent, gram = call(
-        functools.partial(prepare_kernel, scale, leaf_size),
+    u_row, z_lhs, uz_row, uz_col, sent = call(
+        functools.partial(prepare_kernel, leaf_size),
         [
-            sds((count, 4 * feats), BF16),
             sds((1, count), F32),
             sds((per_device * skel_count, 4 * feats), BF16),
             sds((per_device, skel_count), F32),
             sds((per_device * skel_count, LANES), F32),
             sds((subs, count + (feats // subs) * skel_count), F32),
-            sds((1, LANES), F32),
         ],
-        points,
         qt,
         skeleton,
         rskel,
         current.reshape(1, count),
+        name="prepare",
+    )
+    got = lax.all_to_all(sent, "sub", 0, 0, tiled=True)
+    held, got = lax.optimization_barrier((jnp.stack([low, qt, high]), got))
+    window = lax.all_gather(held, "sub", axis=0)
+    lhs, gram = call(
+        functools.partial(own_kernel, scale),
+        [sds((count, 4 * feats), BF16), sds((1, LANES), F32)],
+        points,
         krylov_basis,
-        name="prepare",
-    )
-    got = lax.all_to_all(sent, "sub", 0, 0, tiled=True)
+        name="own",
+    )
     vec_width = count + per_device * skel_count + skel_count
-    tab_width = vec_width + per_device * skel_count + (feats // subs) * skel_count
-    tree_row, sent = call(
+    skels = per_device * skel_count
+    near_width = count + 2 * skels
+    tree_row, near_row, far_row = call(
         start_kernel,
-        [sds((1, count), F32), sds((1, tab_width), F32)],
+        [
+            sds((1, count), F32),
+            sds((1, near_width), F32),
+            sds((1, skel_count * (1 + feats // subs)), F32),
+        ],
         got,
         order,
         u_row,
@@ -450,7 +463,11 @@
         skeleton,
         name="start",
     )
-    tab = to_all(sent, everyone)
+    near_row, tab = lax.optimization_barrier((near_row, to_all(far_row, everyone)))
+    sides = [lax.ppermute(near_row, "leaf", ring), near_row, lax.ppermute(near_row, "leaf", back)]
+    near_rows = jnp.concatenate(sides, axis=1)
+    near_rows = jnp.broadcast_to(near_rows, (subs, near_rows.shape[1]))
+    near_vec = lax.all_to_all(near_rows, "sub", 0, 0, tiled=True)
     (top,) = call(
         functools.partial(top_kernel, feats),
         [sds((leaves, skel_count, skel_count), F32)],
@@ -484,6 +501,7 @@
         root_maps,
         top,
         tree_row,
+        near_vec,
         tab,
         smem=(0, 1),
         far=(2,),
@@ -496,7 +514,6 @@
             pltpu.SemaphoreType.DMA((subs,)),
             pltpu.SemaphoreType.DMA,
         ],
-        room=58,
         name="first",
     )
     vec = to_all(sent, everyone)
@@ -518,15 +535,13 @@
         tree_row,
         order,
         smem=(0, 1),
-        far=(8,),
-        scratch=[spread, sums, halved, pltpu.SemaphoreType.DMA],
-        room=58,
+        scratch=[spread, sums],
         name="second",
     )
     got = lax.all_to_all(sent, "sub", 0, 0, tiled=True)
     user_row, sent = call(
         project_kernel,
-        [sds((1, count), F32), sds((1, 2 * LANES), F32)],
+        [sds((1, count), F32), sds((1, LANES), F32)],
         got,
         krylov_basis,
         gram,

time: 171 us -> 165 us (0.965)
  waiting for transfers between devices: 36.4 us -> 10.1 us
  blocking collectives: 56.4 us -> 77.7 us
  Pallas kernels: 37.9 us -> 33.5 us
  local copies, waits for them, and re-layouts: 10.1 us -> 12.4 us
    all_to_all x2 -> x3, blocking collectives: 36.6 us -> 59.4 us  [to_all(): lax.all_to_all(jnp.broadcast_to(row, (everyone, row.shape[1])), BOTH, 0,...]
    all_to_all x1, waiting for transfers between devices: 24.6 us -> 3.6 us  [shards(): near_vec = lax.all_to_all(near_rows, 'sub', 0, 0, tiled=True)]
    ppermute x1, waiting for transfers between devices: 5.2 us -> 0.01 us  [shards(): low = lax.ppermute(qt, 'leaf', ring)]
    ppermute x0 -> x2, waiting for transfers between devices: none -> 5.16 us  [the longest x1 4.8 us: shards(): lax.ppermute(near_row, 'leaf', ring)]
    ppermute x1, waiting for transfers between devices: 4.97 us -> 0.01 us  [shards(): high = lax.ppermute(qt, 'leaf', back)]
    pallas_call x7 -> x8, Pallas kernels: 37.9 us -> 33.5 us  [call(): pl.pallas_call(body, out_shape=outs, in_specs=specs, out_specs=[pl.BlockS...]
    unnamed x44 -> x52, local copies, waits for them, and re-layouts: 6.36 us -> 10.2 us
    ppermute x0 -> x2, starting transfers between devices: none -> 1.95 us  [the longest x1 1.95 us: shards(): lax.ppermute(near_row, 'leaf', back)]
  transfers between devices with their start and end apart: 4 -> 6, of which waited for: 4 -> 4; matrix products, arithmetic and copies ran while one was open for 2% -> 1% of each run, Pallas kernels for 2% -> 2%
where the time goes in v4:
time: 165 us; the launch traced here: 164 us
  blocking collectives  77.7 us (47%)
  Pallas kernels  33.5 us (20%)
  between operations  14.3 us (9%)
  starting transfers between devices  13.5 us (8%)
  local copies, waits for them, and re-layouts  12.4 us (8%)
  waiting for transfers between devices  10.1 us (6%)
  other arithmetic  2.84 us (2%)
    all_to_all x3, blocking collectives, to_all(): lax.all_to_all(jnp.broadcast_to(row, (everyone, row.shape[1])), BOTH, 0,...  59.4 us
    pallas_call x8, Pallas kernels, call(): pl.pallas_call(body, out_shape=outs, in_specs=specs, out_specs=[pl.BlockS...  33.5 us
    all_to_all x2, blocking collectives, shards(): got = lax.all_to_all(sent, 'sub', 0, 0, tiled=True)  18.3 us
    unnamed x52, local copies, waits for them, and re-layouts  10.2 us
    ppermute x1, starting transfers between devices, shards(): high = lax.ppermute(qt, 'leaf', back)  6.85 us
    ppermute x1, waiting for transfers between devices, shards(): lax.ppermute(near_row, 'leaf', ring)  4.8 us
    all_to_all x1, starting transfers between devices, shards(): near_vec = lax.all_to_all(near_rows, 'sub', 0, 0, tiled=True)  4.63 us
    all_to_all x1, waiting for transfers between devices, shards(): near_vec = lax.all_to_all(near_rows, 'sub', 0, 0, tiled=True)  3.6 us
  transfers between devices with their start and end apart: 6, of which 4 were waited for; matrix products, arithmetic and copies ran while one was open for 1% of the time, Pallas kernels for 2%

profile of v4, /device:TPU:1, one launch (start us, length us, event | category | flops | bytes accessed | tf_op | source)
XLA Modules:
  0.0 164.3 jit_solution(3410841556989916352)
XLA Ops:
  7.2 1.1 multiply_bitcast_fusion
  8.3 6.8 %collective-permute-start.1 = (f32[64,1024]{1,0:T(8,128)S(1)}, f32[64,1024]{1,0:T(8,128)S(1)}, u32[]{:S(2)}, u32[]{:S(2)}) collective-permute-start(f32[64,1024]{1,0:T(8,128)S(1)} %get-tuple-element.47.qt), channel_id=1, source_target_pairs={{8,0},{16,8},{24,16},{32,24},{40,32},{48,40},{56,48},{64,56},{72,6... | collective-permute-start | bytes 786440 | tf_op jit(solution)/shard_map/ppermute | solution.py:407
  15.2 0.7 broadcast_subtract_fusion.rskel
  15.8 0.7 copy-done.13
  16.5 0.7 copy-done.14
  17.8 10.1 %all_to_all.56 = f32[8,1,2048]{2,1,0:T(1,128)S(1)} all-to-all(f32[8,1,2048]{2,1,0:T(1,128)S(1)} %copy.15), channel_id=1, replica_groups=mesh['leaf'=16,'sub'=8] {'sub'}, dimensions={0} | all-to-all | bytes 131072 | tf_op jit(solution)/shard_map/all_to_all | solution.py:437
  27.9 0.9 pad_maximum_fusion
  28.9 1.0 copy-done.2
  29.9 1.0 copy-done.4
  31.0 0.7 copy-done.11
  31.6 0.7 copy-done.15
  32.3 0.5 start.1
  33.2 22.1 %all_to_all.57 = f32[128,1,1152]{2,1,0:T(1,128)S(1)} all-to-all(f32[128,1,1152]{2,1,0:T(1,128)S(1)} %broadcast_in_dim.11), channel_id=1, replica_groups=mesh['leaf'=16,'sub'=8] {'leaf','sub'}, dimensions={0} | all-to-all | bytes 1179648 | tf_op jit(solution)/shard_map/all_to_all | solution.py:379
  55.4 2.0 %collective-permute-start.3 = (f32[1,1536]{1,0:T(1,128)S(1)}, f32[1,1536]{1,0:T(1,128)S(1)}, u32[]{:S(2)}, u32[]{:S(2)}) collective-permute-start(f32[1,1536]{1,0:T(1,128)S(1)} %get-tuple-element.36), channel_id=1, source_target_pairs={{8,0},{16,8},{24,16},{32,24},{40,32},{48,40},{56,48},{64,56},{72,6... | collective-permute-start | bytes 18440 | tf_op jit(solution)/shard_map/ppermute | solution.py:467
  58.3 4.8 %collective-permute-done.2 = f32[1,1536]{1,0:T(1,128)S(1)} collective-permute-done((f32[1,1536]{1,0:T(1,128)S(1)}, f32[1,1536]{1,0:T(1,128)S(1)}, u32[]{:S(2)}, u32[]{:S(2)}) %collective-permute-start.2) | collective-permute-done | bytes 6176 | tf_op jit(solution)/shard_map/ppermute | solution.py:467
  63.2 0.7 broadcast_in_dim.12
  63.9 4.6 %all-to-all-start.2 = ((f32[8,1,4608]{2,1,0:T(1,128)}), f32[8,1,4608]{2,1,0:T(1,128)S(1)}, u32[]{:S(2)}, u32[]{:S(2)}) async-start(f32[8,1,4608]{2,1,0:T(1,128)} %broadcast_in_dim.12), calls=%async_computation.2 | async-start | bytes 294912 | tf_op jit(solution)/shard_map/all_to_all | solution.py:470
  68.6 2.5 %top.1 = f32[16,128,128]{2,1,0:T(8,128)S(1)} custom-call(s32[5,32]{1,0:T(8,128)S(1)} %fusion.info, f32[128,1152]{1,0:T(8,128)S(1)} %bitcast.33), custom_call_target="tpu_custom_call" | custom-call | tf_op jit(solution)/shard_map/top/pallas_call | solution.py:67
  71.1 1.0 copy-done
  72.1 3.6 %all-to-all-done.2 = f32[8,1,4608]{2,1,0:T(1,128)S(1)} async-done(((f32[8,1,4608]{2,1,0:T(1,128)}), f32[8,1,4608]{2,1,0:T(1,128)S(1)}, u32[]{:S(2)}, u32[]{:S(2)}) %all-to-all-start.2) | async-done | bytes 147488 | tf_op jit(solution)/shard_map/all_to_all | solution.py:470
  75.7 1.3 all-gather.3.cloned.1.call-done
  77.0 0.9 copy-done.10
  77.9 0.7 copy-done.16
  78.6 15.8 %first.1 = (f32[1,1024]{1,0:T(1,128)S(1)}, f32[1,1408]{1,0:T(1,128)S(1)}, bf16[48,128,512]{2,1,0:T(8,128)(2,1)}, f32[8,128,128]{2,1,0:T(8,128)S(1)}) custom-call(s32[5,32]{1,0:T(8,128)S(1)} %fusion.info, f32[2]{0:T(128)S(1)} %copy-done.16, f32[8,3,64,1024]{3,2,1,0:T(8,128)} %bitcast.46, bf16[1024,256]{1,0:T(8,128)(2,1)S(1)} %get-tuple-element.24.lhs, ...), custom_call_target="tpu_custom_call" | custom-call | tf_op jit(solution)/shard_map/first/pallas_call | solution.py:67
  94.4 0.8 copy-done.6
  95.7 23.8 %all_to_all.58 = f32[128,1,1408]{2,1,0:T(1,128)S(1)} all-to-all(f32[128,1,1408]{2,1,0:T(1,128)S(1)} %broadcast_in_dim.26), channel_id=1, replica_groups=mesh['leaf'=16,'sub'=8] {'leaf','sub'}, dimensions={0} | all-to-all | bytes 1441792 | tf_op jit(solution)/shard_map/all_to_all | solution.py:379
  119.5 1.0 copy-done.7
  120.6 0.7 copy-done.17
  121.2 13.1 %second.1 = f32[8,1024]{1,0:T(8,128)S(1)} custom-call(s32[5,32]{1,0:T(8,128)S(1)} %fusion.info, f32[2]{0:T(128)S(1)} %copy-done.17, bf16[1024,256]{1,0:T(8,128)(2,1)S(1)} %get-tuple-element.24.lhs, f32[1,1024]{1,0:T(1,128)S(1)} %get-tuple-element.25.u_row, f32[256,128]{1,0:T(8,128)S(1)} %get-tuple-element.26.uz_col, f32[2,128,512]{2,1,0:T(8,128)S(1)} %copy-done.3, ...), custom_call_target="tpu_custom_call" | custom-call | tf_op jit(solution)/shard_map/second/pallas_call | solution.py:67
  134.4 8.3 %all_to_all.59 = f32[8,1,1024]{2,1,0:T(1,128)S(1)} all-to-all(f32[8,1,1024]{2,1,0:T(1,128)S(1)} %copy.16), channel_id=1, replica_groups=mesh['leaf'=16,'sub'=8] {'sub'}, dimensions={0} | all-to-all | bytes 65536 | tf_op jit(solution)/shard_map/all_to_all | solution.py:541
  142.8 13.5 %all_to_all.60 = f32[128,1,128]{2,1,0:T(1,128)S(1)} all-to-all(f32[128,1,128]{2,1,0:T(1,128)S(1)} %broadcast_in_dim.27), channel_id=1, replica_groups=mesh['leaf'=16,'sub'=8] {'leaf','sub'}, dimensions={0} | all-to-all | bytes 131072 | tf_op jit(solution)/shard_map/all_to_all | solution.py:379
  156.2 0.7 finish.1
  (61 shorter events, 3.3 us)
Async XLA Ops:
  7.2 69.9 %copy-start.5 = (f32[2,128,512]{2,1,0:T(8,128)S(1)}, f32[2,128,512]{2,1,0:T(8,128)}, u32[]{:S(2)}) copy-start(f32[2,128,512]{2,1,0:T(8,128)} %rm.5) | copy-start | bytes 1572868
  7.2 69.8 %copy-start.3 = (f32[2,128,512]{2,1,0:T(8,128)S(1)}, f32[2,128,512]{2,1,0:T(8,128)}, u32[]{:S(2)}) copy-start(f32[2,128,512]{2,1,0:T(8,128)} %lm.5) | copy-start | bytes 1572868
  7.2 50.4 %copy-start.8 = (f32[8,1024]{1,0:T(8,128)S(1)}, f32[8,1024]{1,0:T(8,128)}, u32[]{:S(2)}) copy-start(f32[8,1024]{1,0:T(8,128)} %basis.5) | copy-start | bytes 98308
  7.2 69.8 %all-gather.3.cloned.1.call-start = ((), (), s32[]{:S(2)}) async-start(), calls=%async_computation.6 | async-start | bytes 7077888 | tf_op jit(solution)/shard_map/all_gather | solution.py:439
  8.3 19.6 %collective-permute-start.1 = (f32[64,1024]{1,0:T(8,128)S(1)}, f32[64,1024]{1,0:T(8,128)S(1)}, u32[]{:S(2)}, u32[]{:S(2)}) collective-permute-start(f32[64,1024]{1,0:T(8,128)S(1)} %get-tuple-element.47.qt), channel_id=1, source_target_pairs={{8,0},{16,8},{24,16},{32,24},{40,32},{48,40},{56,48},{64,56},{72,6... | collective-permute-start | bytes 786440 | tf_op jit(solution)/shard_map/ppermute | solution.py:407
  15.2 12.7 %collective-permute-start = (f32[64,1024]{1,0:T(8,128)S(1)}, f32[64,1024]{1,0:T(8,128)S(1)}, u32[]{:S(2)}, u32[]{:S(2)}) collective-permute-start(f32[64,1024]{1,0:T(8,128)S(1)} %get-tuple-element.47.qt), channel_id=1, source_target_pairs={{0,8},{8,16},{16,24},{24,32},{32,40},{40,48},{48,56},{56,64},{64,7... | collective-permute-start | bytes 786440 | tf_op jit(solution)/shard_map/ppermute | solution.py:406
  15.8 0.7 copy-start.13
  16.5 0.7 copy-start.14
  17.2 40.1 %copy-start.20 = (f32[1024,64]{0,1:T(8,128)S(1)}, f32[1024,64]{0,1:T(8,128)}, u32[]{:S(2)}) copy-start(f32[1024,64]{0,1:T(8,128)} %param.11) | copy-start | bytes 786436
  17.2 51.4 %copy-start.21 = (s32[2,4]{1,0:T(2,128)S(1)}, s32[2,4]{1,0:T(2,128)}, u32[]{:S(2)}) copy-start(s32[2,4]{1,0:T(2,128)} %param.21) | copy-start | bytes 100
  17.2 51.4 %copy-start.22 = (s32[2,32]{1,0:T(2,128)S(1)}, s32[2,32]{1,0:T(2,128)}, u32[]{:S(2)}) copy-start(s32[2,32]{1,0:T(2,128)} %param.20) | copy-start | bytes 772
  17.7 10.2 %copy-start.9 = (bf16[256,256]{1,0:T(8,128)(2,1)}, bf16[256,256]{1,0:T(8,128)(2,1)S(1)}, u32[]{:S(2)}) copy-start(bf16[256,256]{1,0:T(8,128)(2,1)S(1)} %get-tuple-element.34.z_lhs) | copy-start | bytes 393220
  28.9 1.0 copy-start.2
  29.9 1.0 copy-start.4
  31.0 0.7 copy-start.11
  31.6 0.7 copy-start.15
  55.4 2.9 %collective-permute-start.3 = (f32[1,1536]{1,0:T(1,128)S(1)}, f32[1,1536]{1,0:T(1,128)S(1)}, u32[]{:S(2)}, u32[]{:S(2)}) collective-permute-start(f32[1,1536]{1,0:T(1,128)S(1)} %get-tuple-element.36), channel_id=1, source_target_pairs={{8,0},{16,8},{24,16},{32,24},{40,32},{48,40},{56,48},{64,56},{72,6... | collective-permute-start | bytes 18440 | tf_op jit(solution)/shard_map/ppermute | solution.py:467
  57.3 5.8 %collective-permute-start.2 = (f32[1,1536]{1,0:T(1,128)S(1)}, f32[1,1536]{1,0:T(1,128)S(1)}, u32[]{:S(2)}, u32[]{:S(2)}) collective-permute-start(f32[1,1536]{1,0:T(1,128)S(1)} %get-tuple-element.36), channel_id=1, source_target_pairs={{0,8},{8,16},{16,24},{24,32},{32,40},{40,48},{48,56},{56,64},{64,7... | collective-permute-start | bytes 18440 | tf_op jit(solution)/shard_map/ppermute | solution.py:467
  58.0 6.0 %copy-start.18 = (f32[1,128]{1,0:T(1,128)}, f32[1,128]{1,0:T(1,128)S(1)}, u32[]{:S(2)}) copy-start(f32[1,128]{1,0:T(1,128)S(1)} %get-tuple-element.41.gram) | copy-start | bytes 1540
  63.9 11.8 %all-to-all-start.2 = ((f32[8,1,4608]{2,1,0:T(1,128)}), f32[8,1,4608]{2,1,0:T(1,128)S(1)}, u32[]{:S(2)}, u32[]{:S(2)}) async-start(f32[8,1,4608]{2,1,0:T(1,128)} %broadcast_in_dim.12), calls=%async_computation.2 | async-start | bytes 294912 | tf_op jit(solution)/shard_map/all_to_all | solution.py:470
  71.1 1.0 copy-start
  77.0 0.9 copy-start.10
  77.9 0.7 copy-start.16
  78.6 40.9 %copy-start.1 = (f32[16,128,128]{2,1,0:T(8,128)S(1)}, f32[16,128,128]{2,1,0:T(8,128)}, u32[]{:S(2)}) copy-start(f32[16,128,128]{2,1,0:T(8,128)} %copy-done) | copy-start | bytes 3145732
  78.6 40.9 %copy-start.12 = (s32[1024]{0:T(1024)S(1)}, s32[1024]{0:T(1024)}, u32[]{:S(2)}) copy-start(s32[1024]{0:T(1024)} %param.17) | copy-start | bytes 12292
  94.4 0.8 copy-start.6
  119.4 23.2 %copy-start.19 = (f32[1,128]{1,0:T(1,128)S(1)}, f32[1,128]{1,0:T(1,128)}, u32[]{:S(2)}) copy-start(f32[1,128]{1,0:T(1,128)} %copy-done.18) | copy-start | bytes 1540
  119.5 1.0 copy-start.7
  120.6 0.7 copy-start.17
Sparse Core Ops, SparseCore 0:
  29.0 47.9 all-gather.2

commit v5 on v4

--- a/solution.py
+++ b/solution.py
@@ -270,9 +270,19 @@
     return jnp.concatenate(outs, axis=1)
 
 
+def bring(sources, targets, sems):
+    copies = [
+        pltpu.make_async_copy(src, dst, sems.at[n]) for n, (src, dst) in enumerate(zip(sources, targets))
+    ]
+    for copy in copies:
+        copy.start()
+    return copies
+
+
 def first_kernel(
-    counts, info, ritz, window, lhs, z_lhs, u_row, uz_row, uz_col, lm, rm, top, v_row, vec, tab,
-    first_row, sent, split_out, far_blocks, landed, split, values, acc, sems, out_sem,
+    counts, info, ritz, window, lhs, z_in, u_row, uz_row, uz_col, lm_in, rm_in, top_in, v_row, vec, tab_in,
+    first_row, sent, split_out, far_blocks,
+    landed, split, values, acc, z_lhs, lm, rm, top, tab, sems, late_sems, out_sem,
 ):
     near_count, far_count = counts
     per_device, skel_count, leaf_size = lm.shape
@@ -281,6 +291,7 @@
     copies = [pltpu.make_async_copy(window.at[d], landed.at[d], sems.at[d]) for d in range(subs)]
     for copy in copies:
         copy.start()
+    late = bring((z_in, top_in, tab_in, lm_in, rm_in), (z_lhs, top, tab, lm, rm), late_sems)
     width = vec.shape[1] // sides
     skels = per_device * skel_count
 
@@ -288,7 +299,6 @@
         return [vec[:, side * width + start : side * width + start + size] for side in range(sides)]
 
     spread_values(sides_of(0, count), values)
-    root_out = top_sums(top, tab, subs, 0)
     for d in range(subs):
         copies[d].wait()
         for side in range(sides):
@@ -300,6 +310,9 @@
     written = pltpu.make_async_copy(split, split_out, out_sem)
     written.start()
     near_sums(info, split, values, lhs, acc, near_count)
+    for copy in late:
+        copy.wait()
+    root_out = top_sums(top, tab, subs, 0)
     indices = sides_of(count + skels, skels)
     for a in range(per_device):
         for n in range(far_count):
@@ -432,6 +445,7 @@
         skeleton,
         rskel,
         current.reshape(1, count),
+        room=62,
         name="prepare",
     )
     got = lax.all_to_all(sent, "sub", 0, 0, tiled=True)
@@ -461,6 +475,7 @@
         leaf_maps,
         root_maps,
         skeleton,
+        room=62,
         name="start",
     )
     near_row, tab = lax.optimization_barrier((near_row, to_all(far_row, everyone)))
@@ -480,6 +495,8 @@
     counts = (near_count, far_count)
     spread = pltpu.VMEM((slots, 8, leaf_size), F32)
     sums = pltpu.VMEM((count, LANES), F32)
+    maps = pltpu.VMEM(leaf_maps.shape, F32)
+    tops = pltpu.VMEM(top.shape, F32)
     halved = pltpu.VMEM((slots, 2 * feats, leaf_size), BF16)
     first_row, sent, split, far_blocks = call(
         functools.partial(first_kernel, counts),
@@ -504,14 +521,20 @@
         near_vec,
         tab,
         smem=(0, 1),
-        far=(2,),
+        far=(2, 4, 8, 9, 10, 13),
         hbm_outs=(2,),
         scratch=[
             pltpu.VMEM(window.shape, F32),
             halved,
             spread,
             sums,
+            pltpu.VMEM(z_lhs.shape, BF16),
+            maps,
+            maps,
+            tops,
+            pltpu.VMEM(tab.shape, F32),
             pltpu.SemaphoreType.DMA((subs,)),
+            pltpu.SemaphoreType.DMA((5,)),
             pltpu.SemaphoreType.DMA,
         ],
         name="first",

time: 165 us -> 168 us (1.018)
  other arithmetic: 2.84 us -> 5.77 us
  Pallas kernels: 33.5 us -> 36.4 us
  local copies, waits for them, and re-layouts: 12.4 us -> 10 us
    unnamed x52 -> x46, local copies, waits for them, and re-layouts: 10.2 us -> 7.01 us
    pallas_call x8, Pallas kernels: 33.5 us -> 36.4 us  [call(): pl.pallas_call(body, out_shape=outs, in_specs=specs, out_specs=[pl.BlockS...]
  transfers between devices with their start and end apart: 6 -> 6, of which waited for: 4 -> 3; matrix products, arithmetic and copies ran while one was open for 1% -> 4% of each run, Pallas kernels for 2% -> 4%
where the time goes in v5:
time: 168 us; the launch traced here: 167 us
  blocking collectives  77.1 us (46%)
  Pallas kernels  36.4 us (22%)
  between operations  14.3 us (9%)
  starting transfers between devices  13.6 us (8%)
  local copies, waits for them, and re-layouts  10 us (6%)
  waiting for transfers between devices  9.81 us (6%)
  other arithmetic  5.77 us (3%)
    all_to_all x3, blocking collectives, to_all(): lax.all_to_all(jnp.broadcast_to(row, (everyone, row.shape[1])), BOTH, 0,...  58.8 us
    pallas_call x8, Pallas kernels, call(): pl.pallas_call(body, out_shape=outs, in_specs=specs, out_specs=[pl.BlockS...  36.4 us
    all_to_all x2, blocking collectives, shards(): got = lax.all_to_all(sent, 'sub', 0, 0, tiled=True)  18.3 us
    unnamed x46, local copies, waits for them, and re-layouts  7.01 us
    ppermute x1, starting transfers between devices, shards(): high = lax.ppermute(qt, 'leaf', back)  6.85 us
    all_to_all x1, starting transfers between devices, shards(): near_vec = lax.all_to_all(near_rows, 'sub', 0, 0, tiled=True)  4.67 us
    ppermute x1, waiting for transfers between devices, shards(): lax.ppermute(near_row, 'leaf', ring)  4.41 us
    all_to_all x1, waiting for transfers between devices, shards(): near_vec = lax.all_to_all(near_rows, 'sub', 0, 0, tiled=True)  3.7 us
  transfers between devices with their start and end apart: 6, of which 3 were waited for; matrix products, arithmetic and copies ran while one was open for 4% of the time, Pallas kernels for 4%

profile of v5, /device:TPU:1, one launch (start us, length us, event | category | flops | bytes accessed | tf_op | source)
XLA Modules:
  0.0 167.0 jit_solution(12068309600315554448)
XLA Ops:
  7.3 1.1 multiply_bitcast_fusion
  8.4 6.8 %collective-permute-start.1 = (f32[64,1024]{1,0:T(8,128)S(1)}, f32[64,1024]{1,0:T(8,128)}, u32[]{:S(2)}, u32[]{:S(2)}) collective-permute-start(f32[64,1024]{1,0:T(8,128)S(1)} %get-tuple-element.47.qt), channel_id=1, source_target_pairs={{8,0},{16,8},{24,16},{32,24},{40,32},{48,40},{56,48},{64,56},{72,6... | collective-permute-start | bytes 786440 | tf_op jit(solution)/shard_map/ppermute | solution.py:420
  15.2 1.2 broadcast_subtract_fusion.rskel
  16.4 2.1 %prepare.1 = (f32[1,1024]{1,0:T(1,128)}, bf16[256,256]{1,0:T(8,128)(2,1)}, f32[2,128]{1,0:T(2,128)}, f32[256,128]{1,0:T(8,128)}, f32[8,2048]{1,0:T(8,128)}) custom-call(f32[64,1024]{1,0:T(8,128)} %copy-done.17, s32[2,128]{1,0:T(2,128)} %skel.3, s32[1,128]{1,0:T(1,128)} %broadcast_subtract_fusion.rskel, f32[1,1024]{1,0:T(1,128)} %bitcast.46), custom_call_target="tpu_custom_call" | custom-call | tf_op jit(solution)/shard_map/prepare/pallas_call | solution.py:67
  18.5 0.9 copy.15
  19.5 10.1 %all_to_all.56 = f32[8,1,2048]{2,1,0:T(1,128)S(1)} all-to-all(f32[8,1,2048]{2,1,0:T(1,128)S(1)} %copy.15), channel_id=1, replica_groups=mesh['leaf'=16,'sub'=8] {'sub'}, dimensions={0} | all-to-all | bytes 131072 | tf_op jit(solution)/shard_map/all_to_all | solution.py:451
  29.5 0.6 copy.30
  30.2 2.0 %pad_maximum_fusion = f32[3,64,1024]{2,1,0:T(8,128)} fusion(f32[1,64,1024]{2,1,0:T(8,128)} %bitcast.4, f32[1,64,1024]{2,1,0:T(8,128)S(1)} %get-tuple-element.46, f32[1,64,1024]{2,1,0:T(8,128)} %bitcast.2), kind=kLoop, calls=%fused_computation | loop fusion | flops 393216 | bytes 1572864 | tf_op jit(solution)/shard_map/stack | solution.py:452
  32.2 2.4 %start.1 = (f32[1,1024]{1,0:T(1,128)}, f32[1,1536]{1,0:T(1,128)}, f32[1,1152]{1,0:T(1,128)}) custom-call(f32[8,2048]{1,0:T(8,128)} %bitcast.44, s32[1,1024]{1,0:T(1,128)} %bitcast.40, f32[1,1024]{1,0:T(1,128)} %get-tuple-element.25.u_row, f32[2,128]{1,0:T(2,128)} %get-tuple-element.29.uz_row, f32[2,128,512]{2,1,0:T(8,128)} %lm.3, f32[2,128,512]{2,1,0:T(8,128)} %rm.3, ...), custom_call_target="tpu_custom_call" | custom-call | tf_op jit(solution)/shard_map/start/pallas_call | solution.py:67
  34.6 0.7 reduce
  35.6 21.8 %all_to_all.57 = f32[128,1,1152]{2,1,0:T(1,128)S(1)} all-to-all(f32[128,1,1152]{2,1,0:T(1,128)S(1)} %broadcast_in_dim.11), channel_id=1, replica_groups=mesh['leaf'=16,'sub'=8] {'leaf','sub'}, dimensions={0} | all-to-all | bytes 1179648 | tf_op jit(solution)/shard_map/all_to_all | solution.py:392
  57.4 2.1 %collective-permute-start.3 = (f32[1,1536]{1,0:T(1,128)}, f32[1,1536]{1,0:T(1,128)S(1)}, u32[]{:S(2)}, u32[]{:S(2)}) collective-permute-start(f32[1,1536]{1,0:T(1,128)} %get-tuple-element.36), channel_id=1, source_target_pairs={{8,0},{16,8},{24,16},{32,24},{40,32},{48,40},{56,48},{64,56},{72,6... | collective-permute-start | bytes 18440 | tf_op jit(solution)/shard_map/ppermute | solution.py:482
  59.5 1.1 copy.14.pts
  61.0 4.4 %collective-permute-done.2 = f32[1,1536]{1,0:T(1,128)S(1)} collective-permute-done((f32[1,1536]{1,0:T(1,128)}, f32[1,1536]{1,0:T(1,128)S(1)}, u32[]{:S(2)}, u32[]{:S(2)}) %collective-permute-start.2) | collective-permute-done | bytes 6176 | tf_op jit(solution)/shard_map/ppermute | solution.py:482
  65.5 0.7 maximum_reduce_fusion
  66.2 0.7 broadcast_in_dim.12
  66.9 4.7 %all-to-all-start.2 = ((f32[8,1,4608]{2,1,0:T(1,128)}), f32[8,1,4608]{2,1,0:T(1,128)S(1)}, u32[]{:S(2)}, u32[]{:S(2)}) async-start(f32[8,1,4608]{2,1,0:T(1,128)} %broadcast_in_dim.12), calls=%async_computation.2 | async-start | bytes 294912 | tf_op jit(solution)/shard_map/all_to_all | solution.py:485
  71.7 2.5 %top.1.top_in = f32[16,128,128]{2,1,0:T(8,128)S(1)} custom-call(s32[5,32]{1,0:T(8,128)S(1)} %fusion.info, f32[128,1152]{1,0:T(8,128)S(1)} %bitcast.33), custom_call_target="tpu_custom_call" | custom-call | tf_op jit(solution)/shard_map/top/pallas_call | solution.py:67
  74.2 1.0 copy-done
  75.2 3.7 %all-to-all-done.2 = f32[8,1,4608]{2,1,0:T(1,128)S(1)} async-done(((f32[8,1,4608]{2,1,0:T(1,128)}), f32[8,1,4608]{2,1,0:T(1,128)S(1)}, u32[]{:S(2)}, u32[]{:S(2)}) %all-to-all-start.2) | async-done | bytes 147488 | tf_op jit(solution)/shard_map/all_to_all | solution.py:485
  78.9 1.7 all-gather.3.cloned.1.call-done
  80.6 0.9 copy-done.8
  81.5 0.7 copy-done.13
  82.2 15.2 %first.1 = (f32[1,1024]{1,0:T(1,128)S(1)}, f32[1,1408]{1,0:T(1,128)S(1)}, bf16[48,128,512]{2,1,0:T(8,128)(2,1)}, f32[8,128,128]{2,1,0:T(8,128)S(1)}) custom-call(s32[5,32]{1,0:T(8,128)S(1)} %fusion.info, f32[2]{0:T(128)S(1)} %copy-done.13, f32[8,3,64,1024]{3,2,1,0:T(8,128)} %bitcast.43, bf16[1024,256]{1,0:T(8,128)(2,1)S(1)} %get-tuple-element.24.lhs, ...), custom_call_target="tpu_custom_call" | custom-call | tf_op jit(solution)/shard_map/first/pallas_call | solution.py:67
  97.4 0.8 copy-done.5
  98.6 23.5 %all_to_all.58 = f32[128,1,1408]{2,1,0:T(1,128)S(1)} all-to-all(f32[128,1,1408]{2,1,0:T(1,128)S(1)} %broadcast_in_dim.26), channel_id=1, replica_groups=mesh['leaf'=16,'sub'=8] {'leaf','sub'}, dimensions={0} | all-to-all | bytes 1441792 | tf_op jit(solution)/shard_map/all_to_all | solution.py:392
  122.2 1.0 copy-done.6
  123.2 0.7 copy-done.14
  123.9 13.1 %second.1 = f32[8,1024]{1,0:T(8,128)S(1)} custom-call(s32[5,32]{1,0:T(8,128)S(1)} %fusion.info, f32[2]{0:T(128)S(1)} %copy-done.14, bf16[1024,256]{1,0:T(8,128)(2,1)S(1)} %get-tuple-element.24.lhs, f32[1,1024]{1,0:T(1,128)S(1)} %copy-done.9, f32[256,128]{1,0:T(8,128)S(1)} %copy-done.4, f32[2,128,512]{2,1,0:T(8,128)S(1)} %copy-done.2, ...), custom_call_target="tpu_custom_call" | custom-call | tf_op jit(solution)/shard_map/second/pallas_call | solution.py:67
  137.0 8.3 %all_to_all.59 = f32[8,1,1024]{2,1,0:T(1,128)S(1)} all-to-all(f32[8,1,1024]{2,1,0:T(1,128)S(1)} %copy.16), channel_id=1, replica_groups=mesh['leaf'=16,'sub'=8] {'sub'}, dimensions={0} | all-to-all | bytes 65536 | tf_op jit(solution)/shard_map/all_to_all | solution.py:564
  145.4 13.5 %all_to_all.60 = f32[128,1,128]{2,1,0:T(1,128)S(1)} all-to-all(f32[128,1,128]{2,1,0:T(1,128)S(1)} %broadcast_in_dim.27), channel_id=1, replica_groups=mesh['leaf'=16,'sub'=8] {'leaf','sub'}, dimensions={0} | all-to-all | bytes 131072 | tf_op jit(solution)/shard_map/all_to_all | solution.py:392
  158.9 0.7 finish.1
  (55 shorter events, 2.1 us)
Async XLA Ops:
  7.2 73.4 %copy-start.3 = (f32[2,128,512]{2,1,0:T(8,128)S(1)}, f32[2,128,512]{2,1,0:T(8,128)}, u32[]{:S(2)}) copy-start(f32[2,128,512]{2,1,0:T(8,128)} %rm.3) | copy-start | bytes 1572868
  7.2 73.4 %copy-start.2 = (f32[2,128,512]{2,1,0:T(8,128)S(1)}, f32[2,128,512]{2,1,0:T(8,128)}, u32[]{:S(2)}) copy-start(f32[2,128,512]{2,1,0:T(8,128)} %lm.3) | copy-start | bytes 1572868
  7.2 53.5 %copy-start.7 = (f32[8,1024]{1,0:T(8,128)S(1)}, f32[8,1024]{1,0:T(8,128)}, u32[]{:S(2)}) copy-start(f32[8,1024]{1,0:T(8,128)} %basis.5) | copy-start | bytes 98308
  7.2 64.4 %copy-start.18 = (s32[2,4]{1,0:T(2,128)S(1)}, s32[2,4]{1,0:T(2,128)}, u32[]{:S(2)}) copy-start(s32[2,4]{1,0:T(2,128)} %param.21) | copy-start | bytes 100
  7.2 64.4 %copy-start.19 = (s32[2,32]{1,0:T(2,128)S(1)}, s32[2,32]{1,0:T(2,128)}, u32[]{:S(2)}) copy-start(s32[2,32]{1,0:T(2,128)} %param.20) | copy-start | bytes 772
  7.2 73.3 %all-gather.3.cloned.1.call-start = ((), (), s32[]{:S(2)}) async-start(), calls=%async_computation.6 | async-start | bytes 7077888 | tf_op jit(solution)/shard_map/all_gather | solution.py:453
  8.4 8.0 %copy-start.17 = (f32[64,1024]{1,0:T(8,128)}, f32[64,1024]{1,0:T(8,128)S(1)}, u32[]{:S(2)}) copy-start(f32[64,1024]{1,0:T(8,128)S(1)} %get-tuple-element.47.qt) | copy-start | bytes 786436
  8.4 21.8 %collective-permute-start.1 = (f32[64,1024]{1,0:T(8,128)S(1)}, f32[64,1024]{1,0:T(8,128)}, u32[]{:S(2)}, u32[]{:S(2)}) collective-permute-start(f32[64,1024]{1,0:T(8,128)S(1)} %get-tuple-element.47.qt), channel_id=1, source_target_pairs={{8,0},{16,8},{24,16},{32,24},{40,32},{48,40},{56,48},{64,56},{72,6... | collective-permute-start | bytes 786440 | tf_op jit(solution)/shard_map/ppermute | solution.py:420
  15.2 15.0 %collective-permute-start = (f32[64,1024]{1,0:T(8,128)S(1)}, f32[64,1024]{1,0:T(8,128)}, u32[]{:S(2)}, u32[]{:S(2)}) collective-permute-start(f32[64,1024]{1,0:T(8,128)S(1)} %get-tuple-element.47.qt), channel_id=1, source_target_pairs={{0,8},{8,16},{16,24},{24,32},{32,40},{40,48},{48,56},{56,64},{64,7... | collective-permute-start | bytes 786440 | tf_op jit(solution)/shard_map/ppermute | solution.py:419
  18.5 62.1 %copy-start.4 = (f32[256,128]{1,0:T(8,128)S(1)}, f32[256,128]{1,0:T(8,128)}, u32[]{:S(2)}) copy-start(f32[256,128]{1,0:T(8,128)} %get-tuple-element.26.uz_col) | copy-start | bytes 393220
  18.5 62.1 %copy-start.9 = (f32[1,1024]{1,0:T(1,128)S(1)}, f32[1,1024]{1,0:T(1,128)}, u32[]{:S(2)}) copy-start(f32[1,1024]{1,0:T(1,128)} %get-tuple-element.25.u_row) | copy-start | bytes 12292
  18.5 62.1 %copy-start.12 = (f32[2,128]{1,0:T(2,128)S(1)}, f32[2,128]{1,0:T(2,128)}, u32[]{:S(2)}) copy-start(f32[2,128]{1,0:T(2,128)} %get-tuple-element.29.uz_row) | copy-start | bytes 3076
  34.6 46.0 %copy-start.11 = (f32[1,1024]{1,0:T(1,128)S(1)}, f32[1,1024]{1,0:T(1,128)}, u32[]{:S(2)}) copy-start(f32[1,1024]{1,0:T(1,128)} %get-tuple-element.35.v_row.tree_row) | copy-start | bytes 12292
  57.4 3.6 %collective-permute-start.3 = (f32[1,1536]{1,0:T(1,128)}, f32[1,1536]{1,0:T(1,128)S(1)}, u32[]{:S(2)}, u32[]{:S(2)}) collective-permute-start(f32[1,1536]{1,0:T(1,128)} %get-tuple-element.36), channel_id=1, source_target_pairs={{8,0},{16,8},{24,16},{32,24},{40,32},{48,40},{56,48},{64,56},{72,6... | collective-permute-start | bytes 18440 | tf_op jit(solution)/shard_map/ppermute | solution.py:482
  59.4 6.0 %collective-permute-start.2 = (f32[1,1536]{1,0:T(1,128)}, f32[1,1536]{1,0:T(1,128)S(1)}, u32[]{:S(2)}, u32[]{:S(2)}) collective-permute-start(f32[1,1536]{1,0:T(1,128)} %get-tuple-element.36), channel_id=1, source_target_pairs={{0,8},{8,16},{16,24},{24,32},{32,40},{40,48},{48,56},{56,64},{64,7... | collective-permute-start | bytes 18440 | tf_op jit(solution)/shard_map/ppermute | solution.py:482
  61.0 5.9 %copy-start.15 = (f32[1,128]{1,0:T(1,128)}, f32[1,128]{1,0:T(1,128)S(1)}, u32[]{:S(2)}) copy-start(f32[1,128]{1,0:T(1,128)S(1)} %get-tuple-element.41.gram) | copy-start | bytes 1540
  66.9 11.9 %all-to-all-start.2 = ((f32[8,1,4608]{2,1,0:T(1,128)}), f32[8,1,4608]{2,1,0:T(1,128)S(1)}, u32[]{:S(2)}, u32[]{:S(2)}) async-start(f32[8,1,4608]{2,1,0:T(1,128)} %broadcast_in_dim.12), calls=%async_computation.2 | async-start | bytes 294912 | tf_op jit(solution)/shard_map/all_to_all | solution.py:485
  74.2 1.0 copy-start
  80.6 0.9 copy-start.8
  81.5 0.7 copy-start.13
  82.2 40.0 %copy-start.1 = (f32[16,128,128]{2,1,0:T(8,128)S(1)}, f32[16,128,128]{2,1,0:T(8,128)}, u32[]{:S(2)}) copy-start(f32[16,128,128]{2,1,0:T(8,128)} %copy-done) | copy-start | bytes 3145732
  82.2 40.0 %copy-start.10 = (s32[1024]{0:T(1024)S(1)}, s32[1024]{0:T(1024)}, u32[]{:S(2)}) copy-start(s32[1024]{0:T(1024)} %param.17) | copy-start | bytes 12292
  97.4 0.8 copy-start.5
  122.1 23.2 %copy-start.16 = (f32[1,128]{1,0:T(1,128)S(1)}, f32[1,128]{1,0:T(1,128)}, u32[]{:S(2)}) copy-start(f32[1,128]{1,0:T(1,128)} %copy-done.15) | copy-start | bytes 1540
  122.2 1.0 copy-start.6
  123.2 0.7 copy-start.14
Sparse Core Ops, SparseCore 0:
  32.3 48.2 all-gather.2

commit v6 on v5

--- a/solution.py
+++ b/solution.py
@@ -445,7 +445,6 @@
         skeleton,
         rskel,
         current.reshape(1, count),
-        room=62,
         name="prepare",
     )
     got = lax.all_to_all(sent, "sub", 0, 0, tiled=True)
@@ -475,7 +474,6 @@
         leaf_maps,
         root_maps,
         skeleton,
-        room=62,
         name="start",
     )
     near_row, tab = lax.optimization_barrier((near_row, to_all(far_row, everyone)))

time: 168 us -> 164 us (0.976)
  Pallas kernels: 36.4 us -> 32.9 us
  other arithmetic: 5.77 us -> 2.84 us
  local copies, waits for them, and re-layouts: 10 us -> 12.4 us
    pallas_call x8, Pallas kernels: 36.4 us -> 32.9 us  [call(): pl.pallas_call(body, out_shape=outs, in_specs=specs, out_specs=[pl.BlockS...]
    unnamed x46 -> x52, local copies, waits for them, and re-layouts: 7.01 us -> 10.2 us
  transfers between devices with their start and end apart: 6 -> 6, of which waited for: 3 -> 4; matrix products, arithmetic and copies ran while one was open for 4% -> 1% of each run, Pallas kernels for 4% -> 2%
where the time goes in v6:
time: 164 us
  blocking collectives  77.7 us (47%)
  Pallas kernels  32.9 us (20%)
  between operations  14.3 us (9%)
  starting transfers between devices  13.5 us (8%)
  local copies, waits for them, and re-layouts  12.4 us (8%)
  waiting for transfers between devices  10.1 us (6%)
  other arithmetic  2.84 us (2%)
    all_to_all x3, blocking collectives, to_all(): lax.all_to_all(jnp.broadcast_to(row, (everyone, row.shape[1])), BOTH, 0,...  59.4 us
    pallas_call x8, Pallas kernels, call(): pl.pallas_call(body, out_shape=outs, in_specs=specs, out_specs=[pl.BlockS...  32.9 us
    all_to_all x2, blocking collectives, shards(): got = lax.all_to_all(sent, 'sub', 0, 0, tiled=True)  18.3 us
    unnamed x52, local copies, waits for them, and re-layouts  10.2 us
    ppermute x1, starting transfers between devices, shards(): high = lax.ppermute(qt, 'leaf', back)  6.85 us
    ppermute x1, waiting for transfers between devices, shards(): lax.ppermute(near_row, 'leaf', ring)  4.8 us
    all_to_all x1, starting transfers between devices, shards(): near_vec = lax.all_to_all(near_rows, 'sub', 0, 0, tiled=True)  4.63 us
    all_to_all x1, waiting for transfers between devices, shards(): near_vec = lax.all_to_all(near_rows, 'sub', 0, 0, tiled=True)  3.6 us
  transfers between devices with their start and end apart: 6, of which 4 were waited for; matrix products, arithmetic and copies ran while one was open for 1% of the time, Pallas kernels for 2%

profile of v6, /device:TPU:1, one launch (start us, length us, event | category | flops | bytes accessed | tf_op | source)
XLA Modules:
  0.0 163.7 jit_solution(1814903199730331298)
XLA Ops:
  7.2 1.1 multiply_bitcast_fusion
  8.3 6.8 %collective-permute-start.1 = (f32[64,1024]{1,0:T(8,128)S(1)}, f32[64,1024]{1,0:T(8,128)S(1)}, u32[]{:S(2)}, u32[]{:S(2)}) collective-permute-start(f32[64,1024]{1,0:T(8,128)S(1)} %get-tuple-element.47.qt), channel_id=1, source_target_pairs={{8,0},{16,8},{24,16},{32,24},{40,32},{48,40},{56,48},{64,56},{72,6... | collective-permute-start | bytes 786440 | tf_op jit(solution)/shard_map/ppermute | solution.py:420
  15.2 0.7 broadcast_subtract_fusion.rskel
  15.8 0.7 copy-done.13
  16.5 0.7 copy-done.14
  17.8 10.1 %all_to_all.56 = f32[8,1,2048]{2,1,0:T(1,128)S(1)} all-to-all(f32[8,1,2048]{2,1,0:T(1,128)S(1)} %copy.15), channel_id=1, replica_groups=mesh['leaf'=16,'sub'=8] {'sub'}, dimensions={0} | all-to-all | bytes 131072 | tf_op jit(solution)/shard_map/all_to_all | solution.py:450
  27.9 0.9 pad_maximum_fusion
  28.9 1.0 copy-done.2
  29.9 1.0 copy-done.4
  31.0 0.7 copy-done.11
  31.6 0.7 copy-done.15
  32.3 0.5 start.1
  33.2 22.1 %all_to_all.57 = f32[128,1,1152]{2,1,0:T(1,128)S(1)} all-to-all(f32[128,1,1152]{2,1,0:T(1,128)S(1)} %broadcast_in_dim.11), channel_id=1, replica_groups=mesh['leaf'=16,'sub'=8] {'leaf','sub'}, dimensions={0} | all-to-all | bytes 1179648 | tf_op jit(solution)/shard_map/all_to_all | solution.py:392
  55.4 2.0 %collective-permute-start.3 = (f32[1,1536]{1,0:T(1,128)S(1)}, f32[1,1536]{1,0:T(1,128)S(1)}, u32[]{:S(2)}, u32[]{:S(2)}) collective-permute-start(f32[1,1536]{1,0:T(1,128)S(1)} %get-tuple-element.36), channel_id=1, source_target_pairs={{8,0},{16,8},{24,16},{32,24},{40,32},{48,40},{56,48},{64,56},{72,6... | collective-permute-start | bytes 18440 | tf_op jit(solution)/shard_map/ppermute | solution.py:480
  58.3 4.8 %collective-permute-done.2 = f32[1,1536]{1,0:T(1,128)S(1)} collective-permute-done((f32[1,1536]{1,0:T(1,128)S(1)}, f32[1,1536]{1,0:T(1,128)S(1)}, u32[]{:S(2)}, u32[]{:S(2)}) %collective-permute-start.2) | collective-permute-done | bytes 6176 | tf_op jit(solution)/shard_map/ppermute | solution.py:480
  63.2 0.7 broadcast_in_dim.12
  63.9 4.6 %all-to-all-start.2 = ((f32[8,1,4608]{2,1,0:T(1,128)}), f32[8,1,4608]{2,1,0:T(1,128)S(1)}, u32[]{:S(2)}, u32[]{:S(2)}) async-start(f32[8,1,4608]{2,1,0:T(1,128)} %broadcast_in_dim.12), calls=%async_computation.2 | async-start | bytes 294912 | tf_op jit(solution)/shard_map/all_to_all | solution.py:483
  68.6 2.5 %top.1.top_in = f32[16,128,128]{2,1,0:T(8,128)S(1)} custom-call(s32[5,32]{1,0:T(8,128)S(1)} %fusion.info, f32[128,1152]{1,0:T(8,128)S(1)} %bitcast.33), custom_call_target="tpu_custom_call" | custom-call | tf_op jit(solution)/shard_map/top/pallas_call | solution.py:67
  71.1 1.0 copy-done
  72.1 3.6 %all-to-all-done.2 = f32[8,1,4608]{2,1,0:T(1,128)S(1)} async-done(((f32[8,1,4608]{2,1,0:T(1,128)}), f32[8,1,4608]{2,1,0:T(1,128)S(1)}, u32[]{:S(2)}, u32[]{:S(2)}) %all-to-all-start.2) | async-done | bytes 147488 | tf_op jit(solution)/shard_map/all_to_all | solution.py:483
  75.7 1.3 all-gather.3.cloned.1.call-done
  77.0 0.9 copy-done.10
  77.9 0.7 copy-done.16
  78.6 15.2 %first.1 = (f32[1,1024]{1,0:T(1,128)S(1)}, f32[1,1408]{1,0:T(1,128)S(1)}, bf16[48,128,512]{2,1,0:T(8,128)(2,1)}, f32[8,128,128]{2,1,0:T(8,128)S(1)}) custom-call(s32[5,32]{1,0:T(8,128)S(1)} %fusion.info, f32[2]{0:T(128)S(1)} %copy-done.16, f32[8,3,64,1024]{3,2,1,0:T(8,128)} %bitcast.46, bf16[1024,256]{1,0:T(8,128)(2,1)S(1)} %get-tuple-element.24.lhs, ...), custom_call_target="tpu_custom_call" | custom-call | tf_op jit(solution)/shard_map/first/pallas_call | solution.py:67
  93.8 0.8 copy-done.6
  95.0 23.8 %all_to_all.58 = f32[128,1,1408]{2,1,0:T(1,128)S(1)} all-to-all(f32[128,1,1408]{2,1,0:T(1,128)S(1)} %broadcast_in_dim.26), channel_id=1, replica_groups=mesh['leaf'=16,'sub'=8] {'leaf','sub'}, dimensions={0} | all-to-all | bytes 1441792 | tf_op jit(solution)/shard_map/all_to_all | solution.py:392
  118.9 1.0 copy-done.7
  119.9 0.7 copy-done.17
  120.6 13.1 %second.1 = f32[8,1024]{1,0:T(8,128)S(1)} custom-call(s32[5,32]{1,0:T(8,128)S(1)} %fusion.info, f32[2]{0:T(128)S(1)} %copy-done.17, bf16[1024,256]{1,0:T(8,128)(2,1)S(1)} %get-tuple-element.24.lhs, f32[1,1024]{1,0:T(1,128)S(1)} %get-tuple-element.25.u_row, f32[256,128]{1,0:T(8,128)S(1)} %get-tuple-element.26.uz_col, f32[2,128,512]{2,1,0:T(8,128)S(1)} %copy-done.3, ...), custom_call_target="tpu_custom_call" | custom-call | tf_op jit(solution)/shard_map/second/pallas_call | solution.py:67
  133.7 8.2 %all_to_all.59 = f32[8,1,1024]{2,1,0:T(1,128)S(1)} all-to-all(f32[8,1,1024]{2,1,0:T(1,128)S(1)} %copy.16), channel_id=1, replica_groups=mesh['leaf'=16,'sub'=8] {'sub'}, dimensions={0} | all-to-all | bytes 65536 | tf_op jit(solution)/shard_map/all_to_all | solution.py:562
  142.1 13.5 %all_to_all.60 = f32[128,1,128]{2,1,0:T(1,128)S(1)} all-to-all(f32[128,1,128]{2,1,0:T(1,128)S(1)} %broadcast_in_dim.27), channel_id=1, replica_groups=mesh['leaf'=16,'sub'=8] {'leaf','sub'}, dimensions={0} | all-to-all | bytes 131072 | tf_op jit(solution)/shard_map/all_to_all | solution.py:392
  155.6 0.7 finish.1
  (61 shorter events, 3.3 us)
Async XLA Ops:
  7.2 69.9 %copy-start.5 = (f32[2,128,512]{2,1,0:T(8,128)S(1)}, f32[2,128,512]{2,1,0:T(8,128)}, u32[]{:S(2)}) copy-start(f32[2,128,512]{2,1,0:T(8,128)} %rm.3) | copy-start | bytes 1572868
  7.2 69.8 %copy-start.3 = (f32[2,128,512]{2,1,0:T(8,128)S(1)}, f32[2,128,512]{2,1,0:T(8,128)}, u32[]{:S(2)}) copy-start(f32[2,128,512]{2,1,0:T(8,128)} %lm.3) | copy-start | bytes 1572868
  7.2 50.4 %copy-start.8 = (f32[8,1024]{1,0:T(8,128)S(1)}, f32[8,1024]{1,0:T(8,128)}, u32[]{:S(2)}) copy-start(f32[8,1024]{1,0:T(8,128)} %basis.5) | copy-start | bytes 98308
  7.2 69.8 %all-gather.3.cloned.1.call-start = ((), (), s32[]{:S(2)}) async-start(), calls=%async_computation.6 | async-start | bytes 7077888 | tf_op jit(solution)/shard_map/all_gather | solution.py:452
  8.3 19.6 %collective-permute-start.1 = (f32[64,1024]{1,0:T(8,128)S(1)}, f32[64,1024]{1,0:T(8,128)S(1)}, u32[]{:S(2)}, u32[]{:S(2)}) collective-permute-start(f32[64,1024]{1,0:T(8,128)S(1)} %get-tuple-element.47.qt), channel_id=1, source_target_pairs={{8,0},{16,8},{24,16},{32,24},{40,32},{48,40},{56,48},{64,56},{72,6... | collective-permute-start | bytes 786440 | tf_op jit(solution)/shard_map/ppermute | solution.py:420
  15.2 12.7 %collective-permute-start = (f32[64,1024]{1,0:T(8,128)S(1)}, f32[64,1024]{1,0:T(8,128)S(1)}, u32[]{:S(2)}, u32[]{:S(2)}) collective-permute-start(f32[64,1024]{1,0:T(8,128)S(1)} %get-tuple-element.47.qt), channel_id=1, source_target_pairs={{0,8},{8,16},{16,24},{24,32},{32,40},{40,48},{48,56},{56,64},{64,7... | collective-permute-start | bytes 786440 | tf_op jit(solution)/shard_map/ppermute | solution.py:419
  15.8 0.7 copy-start.13
  16.5 0.7 copy-start.14
  17.2 40.1 %copy-start.20 = (f32[1024,64]{0,1:T(8,128)S(1)}, f32[1024,64]{0,1:T(8,128)}, u32[]{:S(2)}) copy-start(f32[1024,64]{0,1:T(8,128)} %param.11) | copy-start | bytes 786436
  17.2 51.4 %copy-start.21 = (s32[2,4]{1,0:T(2,128)S(1)}, s32[2,4]{1,0:T(2,128)}, u32[]{:S(2)}) copy-start(s32[2,4]{1,0:T(2,128)} %param.21) | copy-start | bytes 100
  17.2 51.4 %copy-start.22 = (s32[2,32]{1,0:T(2,128)S(1)}, s32[2,32]{1,0:T(2,128)}, u32[]{:S(2)}) copy-start(s32[2,32]{1,0:T(2,128)} %param.20) | copy-start | bytes 772
  17.7 10.2 %copy-start.9 = (bf16[256,256]{1,0:T(8,128)(2,1)}, bf16[256,256]{1,0:T(8,128)(2,1)S(1)}, u32[]{:S(2)}) copy-start(bf16[256,256]{1,0:T(8,128)(2,1)S(1)} %get-tuple-element.34.z_in) | copy-start | bytes 393220
  28.9 1.0 copy-start.2
  29.9 1.0 copy-start.4
  31.0 0.7 copy-start.11
  31.6 0.7 copy-start.15
  55.4 2.9 %collective-permute-start.3 = (f32[1,1536]{1,0:T(1,128)S(1)}, f32[1,1536]{1,0:T(1,128)S(1)}, u32[]{:S(2)}, u32[]{:S(2)}) collective-permute-start(f32[1,1536]{1,0:T(1,128)S(1)} %get-tuple-element.36), channel_id=1, source_target_pairs={{8,0},{16,8},{24,16},{32,24},{40,32},{48,40},{56,48},{64,56},{72,6... | collective-permute-start | bytes 18440 | tf_op jit(solution)/shard_map/ppermute | solution.py:480
  57.3 5.8 %collective-permute-start.2 = (f32[1,1536]{1,0:T(1,128)S(1)}, f32[1,1536]{1,0:T(1,128)S(1)}, u32[]{:S(2)}, u32[]{:S(2)}) collective-permute-start(f32[1,1536]{1,0:T(1,128)S(1)} %get-tuple-element.36), channel_id=1, source_target_pairs={{0,8},{8,16},{16,24},{24,32},{32,40},{40,48},{48,56},{56,64},{64,7... | collective-permute-start | bytes 18440 | tf_op jit(solution)/shard_map/ppermute | solution.py:480
  58.0 6.0 %copy-start.18 = (f32[1,128]{1,0:T(1,128)}, f32[1,128]{1,0:T(1,128)S(1)}, u32[]{:S(2)}) copy-start(f32[1,128]{1,0:T(1,128)S(1)} %get-tuple-element.41.gram) | copy-start | bytes 1540
  63.9 11.8 %all-to-all-start.2 = ((f32[8,1,4608]{2,1,0:T(1,128)}), f32[8,1,4608]{2,1,0:T(1,128)S(1)}, u32[]{:S(2)}, u32[]{:S(2)}) async-start(f32[8,1,4608]{2,1,0:T(1,128)} %broadcast_in_dim.12), calls=%async_computation.2 | async-start | bytes 294912 | tf_op jit(solution)/shard_map/all_to_all | solution.py:483
  71.1 1.0 copy-start
  77.0 0.9 copy-start.10
  77.9 0.7 copy-start.16
  78.6 40.3 %copy-start.1 = (f32[16,128,128]{2,1,0:T(8,128)S(1)}, f32[16,128,128]{2,1,0:T(8,128)}, u32[]{:S(2)}) copy-start(f32[16,128,128]{2,1,0:T(8,128)} %copy-done) | copy-start | bytes 3145732
  78.6 40.3 %copy-start.12 = (s32[1024]{0:T(1024)S(1)}, s32[1024]{0:T(1024)}, u32[]{:S(2)}) copy-start(s32[1024]{0:T(1024)} %param.17) | copy-start | bytes 12292
  93.8 0.8 copy-start.6
  118.8 23.2 %copy-start.19 = (f32[1,128]{1,0:T(1,128)S(1)}, f32[1,128]{1,0:T(1,128)}, u32[]{:S(2)}) copy-start(f32[1,128]{1,0:T(1,128)} %copy-done.18) | copy-start | bytes 1540
  118.9 1.0 copy-start.7
  119.9 0.7 copy-start.17
Sparse Core Ops, SparseCore 0:
  29.0 47.9 all-gather.2
